TPU v7x, 256 devices: a whole 4x4x8 slice. The times are simulated.
256 devices in a mesh: section: 16 (over x, y_lo, core), tensor: 16 (over z, y_hi).
Axes of the slice: x: 4, y: 4 (y_hi: 2, y_lo: 2; y = y_hi * 2 + y_lo), z: 8, core: 2. Of those that a mesh axis runs over, the one named last changes fastest.
Arguments:
- fwd_input: bfloat16 [16, 256, 8192], P('section', 'tensor'), may hold values from -6 to 6
- fwd_segments: int32 [16, 256], P('section'), may hold values from 0 to 3, never falling along the last dimension, each value on 1 to 128 neighbouring positions
- norm_gain: float32 [16, 8192], P('section'), may hold values from 0.25 to 1.75
- w_query: bfloat16 [16, 8192, 4096], P('section', None, 'tensor'), may hold values from -0.0625 to 0.0625
- w_keyval: bfloat16 [16, 2, 8192, 1024], P('section', None, None, 'tensor'), may hold values from -0.0625 to 0.0625
- w_out: bfloat16 [16, 4096, 8192], P('section', 'tensor'), may hold values from -0.09375 to 0.09375
- bwd_grad: bfloat16 [16, 128, 8192], P('section', 'tensor'), may hold values from -6 to 6
- bwd_segments: int32 [16, 128], P('section'), may hold values from 0 to 3, never falling along the last dimension, each value on 1 to 64 neighbouring positions
- parked: bfloat16 [16, 128, 8192], P('section', None, 'tensor'), may hold values from -16 to 16
- parked_input: bfloat16 [16, 128, 8192], P('section', 'tensor'), may hold values from -6 to 6
Outputs:
- received_input: bfloat16 [16, 256, 8192], P('section', 'tensor')
- grad_to_prev: bfloat16 [16, 128, 8192], P('section', 'tensor')
All inputs are finite; a program needn't handle non-finite values.
Results may differ from a plain program's by a relative error of at most 0.018.
Values may be sent and summed in bfloat16 or wider, within the bound.
No kernel may reach another device: no remote copies, remote signals or barrier semaphores. Data moves between devices by JAX's collectives and lax.ppermute only.
A program may use at most 128 MiB of HBM per device.

v0:
```python
import jax
import jax.numpy as jnp
from jax import lax
from jax.experimental import pallas as pl
from jax.experimental.pallas import tpu as pltpu
from jax.sharding import PartitionSpec as P

HD = 128
Q_DEV = 2
RING = 8
STEPS = 8


EPSILON = 1e-05
VMEM_LIMIT = 12 * 1024 * 1024
NEGATIVE = -1e30


def along_z(x, k):
    return lax.ppermute(
        x, "tensor", [(t, (t // 2 + k) % RING * 2 + t % 2) for t in range(2 * RING)]
    )


def across(x):
    return lax.ppermute(x, "tensor", [(t, t ^ 1) for t in range(2 * RING)])


def after(value, *others):
    return lax.optimization_barrier((value, *others))[0]


def lane(move):
    last = []

    def send(x):
        x = after(x, *last)
        last[:] = [move(x)]
        return last[0]

    return send


def lanes():
    return lane(lambda x: along_z(x, 1)), lane(lambda x: along_z(x, -1)), lane(across)


def gather_relative(own, first, parked, mirror):
    up, down, side = lanes()
    a, b = {0: own}, {}
    a[7], a[1], b[0] = up(own), down(own), side(after(own, first))
    a[6], a[2], b[7] = up(a[7]), down(a[1]), side(a[7])
    a[5], a[3], b[2] = up(a[6]), down(a[2]), side(a[2])
    a[4], b[1], b[5] = up(a[5]), down(b[0]), side(a[5])
    saved = lax.ppermute(after(parked, a[5]), "section", mirror)
    a[4], b[1], b[5], saved = lax.optimization_barrier((a[4], b[1], b[5], saved))
    b[6], b[3], b[4] = up(b[7]), down(b[2]), side(a[4])
    return [part[d] for d in range(RING) for part in (a, b)], saved


def z_groups():
    return [[2 * z + column for z in range(RING)] for column in range(2)]


def by_column(column, own, other):
    return jnp.where(column == 0, own, other), jnp.where(column == 0, other, own)


def add_blocks(*terms):
    total = terms[0].astype(jnp.float32)
    for term in terms[1:]:
        total = total + term.astype(jnp.float32)
    return total.astype(jnp.bfloat16)


def onward(x, step, cross):
    sections, devices = lax.axis_size("section"), 2 * RING
    pairs = [
        (s * devices + t, (s + 1) * devices + (((t // 2 + step) % RING * 2 + t % 2) ^ cross))
        for s in range(sections - 1)
        for t in range(devices)
    ]
    return lax.ppermute(x, ("section", "tensor"), pairs)


def scatter_relative(beside, blocks, residual):
    a = {d: blocks[2 * d] for d in range(RING)}
    b = {d: blocks[2 * d + 1] for d in range(RING)}
    up, down, side = lanes()
    from_up, from_down, from_side = down(b[6]), up(b[3]), side(b[4])
    b[7] = add_blocks(b[7], from_up)
    b[2] = add_blocks(b[2], from_down)
    a[4] = add_blocks(a[4], from_side)
    from_up, from_down, from_side = down(a[4]), up(b[1]), side(b[5])
    a[5] = add_blocks(a[5], from_up, from_side)
    b[0] = add_blocks(b[0], from_down)
    a[0] = add_blocks(after(a[0], from_down), residual)
    from_up, from_down, from_side = down(a[5]), up(a[3]), side(b[2])
    a[6] = add_blocks(a[6], from_up)
    a[2] = add_blocks(a[2], from_down, from_side)
    from_up, from_down, from_side = down(a[6]), up(a[2]), side(b[7])
    a[7] = add_blocks(a[7], from_up, from_side)
    a[1] = add_blocks(a[1], from_down)
    last = [onward(after(b[0], from_side), 0, 1)]
    last += [onward(after(a[0], from_side), 0, 0)]
    a[7], a[1], beside = lax.optimization_barrier((a[7], a[1], beside))
    last += [onward(a[7], -1, 0), onward(a[1], 1, 0)]
    return last, beside


def norm_rows(inputs, gain_vector):
    mean_square = jnp.mean(inputs * inputs, axis=-1, keepdims=True)
    return inputs * lax.rsqrt(mean_square + EPSILON) * gain_vector


def exact_dot(a, b, dims):
    return lax.dot_general(
        a,
        b.astype(jnp.float32),
        (dims, ((), ())),
        precision=lax.Precision.HIGHEST,
        preferred_element_type=jnp.float32,
    )


def dot_last(a, b):
    return lax.dot_general(a, b, (((1,), (1,)), ((), ())), preferred_element_type=jnp.float32)


def softmax_rows(scores, allowed):
    masked = jnp.where(allowed, scores, NEGATIVE)
    highest = jnp.max(masked, axis=-1, keepdims=True)
    weights = jnp.exp(masked - highest)
    return weights / jnp.sum(weights, axis=-1, keepdims=True)


def place(shape, axis):
    return lax.broadcasted_iota(jnp.int32, shape, axis)


def turned(row, square):
    same = place(square, 0) == place(square, 1)
    return jnp.sum(jnp.where(same, row, 0.0), axis=1, keepdims=True)


def fetch(source, target, sems, axis):
    size = source.shape[axis] // STEPS
    copies = []
    for i in range(STEPS):
        part = (slice(None), pl.ds(i * size, size)) if axis else (pl.ds(i * size, size),)
        copy = pltpu.make_async_copy(source.at[part], target.at[part], sems.at[i])
        copy.start()
        copies.append(copy)
    return copies


def chunks(width):
    size = width // STEPS
    return [slice(i * size, (i + 1) * size) for i in range(STEPS)]


def backward_kernel(
    where, grads, weight, saved, segments, grad_q, own, other, grads_near, weight_near, sems
):
    grad_copies = fetch(grads, grads_near, sems.at[0], 1)
    copies = fetch(weight, weight_near, sems.at[1], 1)
    tokens = saved.shape[0]
    square = (tokens, tokens)
    scale = HD**-0.5
    key = saved[:, Q_DEV * HD : (Q_DEV + 1) * HD]
    value = saved[:, (Q_DEV + 1) * HD :]
    ids = segments[...].astype(jnp.float32)
    allowed = (place(square, 1) <= place(square, 0)) & (turned(ids, square) == ids)
    heads = [slice(head * HD, (head + 1) * HD) for head in range(Q_DEV)]
    weights = [
        softmax_rows(dot_last(saved[:, part], key) * scale, allowed) for part in heads
    ]
    total = jnp.zeros((tokens, Q_DEV * HD), jnp.float32)
    for part, first, second in zip(chunks(grads.shape[1]), grad_copies, copies):
        first.wait()
        second.wait()
        total += dot_last(grads_near[:, part], weight_near[:, part])
    grad_out = total.astype(jnp.bfloat16)
    grad_key = jnp.zeros((tokens, HD), jnp.float32)
    grad_value = jnp.zeros((tokens, HD), jnp.float32)
    for part, probs in zip(heads, weights):
        query = saved[:, part]
        grad_head = grad_out[:, part]
        grad_probs = dot_last(grad_head, value)
        row_total = jnp.sum(probs * grad_probs, axis=-1, keepdims=True)
        grad_scores = probs * (grad_probs - row_total) * scale
        grad_value += exact_dot(probs.T, grad_head, ((1,), (0,)))
        grad_q[:, part] = exact_dot(grad_scores, key, ((1,), (0,))).astype(jnp.bfloat16)
        grad_key += exact_dot(grad_scores.T, query, ((1,), (0,)))
    half = HD // 2
    low = jnp.concatenate([grad_key[:, :half], grad_value[:, :half]], axis=1)
    high = jnp.concatenate([grad_key[:, half:], grad_value[:, half:]], axis=1)
    even = where[0] % 2 == 0
    own[...] = jnp.where(even, low, high).astype(jnp.bfloat16)
    other[...] = jnp.where(even, high, low).astype(jnp.bfloat16)


def term_kernel(
    grad_q, own, partner, w_query, w_keyval, out, query_near, keyval_near, out_near, sems
):
    query_copies = fetch(w_query, query_near, sems.at[0], 0)
    keyval_copies = fetch(w_keyval, keyval_near, sems.at[1], 1)
    pair = own[...].astype(jnp.float32) + partner[...].astype(jnp.float32)
    pair = pair.astype(jnp.bfloat16)
    writes = []
    for i, part in enumerate(chunks(out.shape[1])):
        query_copies[i].wait()
        keyval_copies[i].wait()
        term = dot_last(grad_q[...], query_near[part, :])
        term += jnp.dot(pair, keyval_near[:, part], preferred_element_type=jnp.float32)
        out_near[:, part] = term.astype(jnp.bfloat16)
        write = pltpu.make_async_copy(out_near.at[:, part], out.at[:, part], sems.at[2, i])
        write.start()
        writes.append(write)
    for write in writes:
        write.wait()


def project_kernel(*refs):
    pieces = refs[: 2 * RING]
    w_query, w_keyval, queries, keyval, query_near, keyval_near, sems = refs[2 * RING :]
    query_copies = fetch(w_query, query_near, sems.at[0], 0)
    keyval_copies = fetch(w_keyval, keyval_near, sems.at[1], 1)
    total_q = jnp.zeros(queries.shape, jnp.float32)
    total_kv = jnp.zeros(keyval.shape, jnp.float32)
    for i, part in enumerate(chunks(w_query.shape[0])):
        rows = jnp.concatenate([piece[:, part] for piece in pieces], axis=0)
        query_copies[i].wait()
        keyval_copies[i].wait()
        total_q += jnp.dot(rows, query_near[part, :], preferred_element_type=jnp.float32)
        total_kv += dot_last(rows, keyval_near[:, part])
    queries[...] = total_q.astype(jnp.bfloat16)
    keyval[...] = total_kv.astype(jnp.bfloat16)


def attend_kernel(where, queries, own, other, segments, weight, *rest):
    outs, (weight_near, sems) = rest[:-2], rest[-2:]
    copies = fetch(weight, weight_near, sems.at[0], 1)
    tokens = queries.shape[0]
    rows = tokens // (2 * RING)
    z, column = where[0] // 2, where[0] % 2

    def token(index):
        chip = (index // (2 * rows) + z) % RING
        side = (index // rows + column) % 2
        return (chip * 2 + side) * rows + index % rows

    square = (tokens, tokens)
    at_col, at_row = token(place((tokens, 1), 0)), token(place((1, tokens), 1))
    ids_row = segments[...].astype(jnp.float32)
    ids_col = turned(ids_row, square)
    of_col = jnp.sum(jnp.where(place(square, 1) == at_col, ids_row, 0.0), axis=1, keepdims=True)
    of_row = jnp.sum(jnp.where(place(square, 0) == at_row, ids_col, 0.0), axis=0, keepdims=True)
    allowed = (at_row <= at_col) & (of_row == of_col)
    theirs = jnp.concatenate(
        [other[(i ^ 1) * rows : ((i ^ 1) + 1) * rows, :] for i in range(2 * RING)], axis=0
    )
    mine = own[...]
    even = column == 0
    low = jnp.where(even, mine, theirs)
    high = jnp.where(even, theirs, mine)
    half = HD // 2
    key = jnp.concatenate([low[:, :half], high[:, :half]], axis=1)
    value = jnp.concatenate([low[:, half:], high[:, half:]], axis=1)
    mixed = []
    for head in range(Q_DEV):
        part = slice(head * HD, (head + 1) * HD)
        scores = dot_last(queries[:, part], key) * HD**-0.5
        probs = softmax_rows(scores, allowed).astype(jnp.bfloat16)
        mixed.append(
            jnp.dot(probs, value, preferred_element_type=jnp.float32).astype(jnp.bfloat16)
        )
    attended = jnp.concatenate(mixed, axis=1)
    for part, copy in zip(chunks(weight.shape[1]), copies):
        copy.wait()
        share = jnp.dot(attended, weight_near[:, part], preferred_element_type=jnp.float32)
        share = share.astype(jnp.bfloat16)
        for i, out in enumerate(outs):
            out[:, part] = share[i * rows : (i + 1) * rows]


def call(kernel, flops, size, outs, in_specs, out_specs, scratch, kind=jax.ShapeDtypeStruct):
    return pl.pallas_call(
        kernel,
        out_shape=[kind(shape, jnp.bfloat16) for shape in outs],
        in_specs=in_specs,
        out_specs=out_specs,
        scratch_shapes=[pltpu.VMEM(shape, jnp.bfloat16) for shape in scratch]
        + [pltpu.SemaphoreType.DMA((3, STEPS))],
        cost_estimate=pl.CostEstimate(flops=flops, bytes_accessed=size, transcendentals=0),
        compiler_params=pltpu.CompilerParams(vmem_limit_bytes=VMEM_LIMIT),
    )


def held():
    return pl.BlockSpec(memory_space=pltpu.VMEM)


def far():
    return pl.BlockSpec(memory_space=pltpu.HBM)


def scalars():
    return pl.BlockSpec(memory_space=pltpu.SMEM)


def local(
    fwd_input,
    fwd_segments,
    norm_gain,
    w_query,
    w_keyval,
    w_out,
    bwd_grad,
    bwd_segments,
    parked,
    parked_input,
):
    sections = lax.axis_size("section")
    tensor_now = lax.axis_index("tensor")
    column = tensor_now % 2
    width = Q_DEV * HD
    gain_vector = norm_gain[0]
    query_weight = w_query[0]
    out_weight = w_out[0]
    features = query_weight.shape[0]
    keyval_weight = jnp.swapaxes(w_keyval[0], 1, 2).reshape(HD, features)
    grad_rows = bwd_grad[0]
    residual = fwd_input[0].astype(jnp.float32)
    normed = norm_rows(residual, gain_vector).astype(jnp.bfloat16)
    fwd_rows, bwd_rows = normed.shape[0], grad_rows.shape[0]
    fwd_tokens, bwd_tokens = fwd_segments.shape[1], bwd_segments.shape[1]
    where_now = jnp.full((1,), tensor_now, jnp.int32)

    mirror = [(s, s ^ sections // 2) for s in range(sections)]
    grad_pair = jnp.concatenate(by_column(column, grad_rows, after(across(grad_rows), normed)), axis=0)
    grads_all = lax.all_gather(grad_pair, "tensor", axis=0, tiled=True, axis_index_groups=z_groups())
    pieces, saved_block = gather_relative(normed, grad_pair, parked[0], mirror)

    grad_query, own_half, other_half = call(
        backward_kernel,
        2 * bwd_tokens * features * width,
        2 * features * (width + bwd_tokens),
        [(bwd_tokens, width), (bwd_tokens, HD), (bwd_tokens, HD)],
        [scalars(), far(), far(), held(), held()],
        [held()] * 3,
        [(bwd_tokens, features), (width, features)],
    )(where_now, grads_all, out_weight, saved_block, bwd_segments)
    pieces, other_half = lax.optimization_barrier((pieces, other_half))
    partner_half = across(other_half)
    saved_rows = lax.ppermute(after(parked_input[0], other_half), "section", mirror)

    queries, own_kv = call(
        project_kernel,
        2 * fwd_tokens * features * (width + HD),
        2 * features * (width + HD + fwd_tokens),
        [(fwd_tokens, width), (fwd_tokens, HD)],
        [held()] * (2 * RING) + [far()] * 2,
        [held()] * 2,
        [(features, width), (HD, features)],
    )(*pieces, query_weight, keyval_weight)
    other_kv = across(own_kv)

    (term,) = call(
        term_kernel,
        2 * bwd_tokens * features * (width + HD),
        2 * features * (width + HD + bwd_tokens),
        [(bwd_tokens, features)],
        [held()] * 3 + [far()] * 2,
        [far()],
        [(features, width), (HD, features), (bwd_tokens, features)],
    )(grad_query, own_half, partner_half, query_weight, keyval_weight)
    pair_sums = lax.psum_scatter(
        term, "tensor", scatter_dimension=0, tiled=True, axis_index_groups=z_groups()
    )

    shares = call(
        attend_kernel,
        2 * fwd_tokens * features * width,
        2 * features * (width + fwd_tokens),
        [(fwd_rows, features)] * (2 * RING),
        [scalars()] + [held()] * 4 + [far()],
        [held()] * (2 * RING),
        [(width, features)],
        pltpu.VMEM,
    )(
        where_now,
        queries,
        own_kv,
        after(other_kv, term, saved_rows),
        fwd_segments,
        out_weight,
    )
    fwd_parts, pair_sums = scatter_relative(pair_sums, shares, residual)

    own_sum, other_sum = by_column(column, pair_sums[:bwd_rows], pair_sums[bwd_rows:])
    grad_normed = own_sum.astype(jnp.float32) + across(other_sum).astype(jnp.float32)
    previous = saved_rows.astype(jnp.float32)
    _, pull_norm = jax.vjp(lambda rows_in: norm_rows(rows_in, gain_vector), previous)
    (grad_norm,) = pull_norm(grad_normed)
    returned = (grad_rows.astype(jnp.float32) + grad_norm).astype(jnp.bfloat16)
    sent_back = lax.ppermute(
        returned, "section", [(s, (s - 1) % sections) for s in range(sections)]
    )
    received = add_blocks(*fwd_parts)
    return (received[None], sent_back[None])


def solution(mesh):
    return jax.shard_map(
        local,
        mesh=mesh,
        in_specs=(
            P("section", "tensor", None),
            P("section", None),
            P("section", None),
            P("section", None, "tensor"),
            P("section", None, None, "tensor"),
            P("section", "tensor", None),
            P("section", "tensor", None),
            P("section", None),
            P("section", None, "tensor"),
            P("section", "tensor", None),
        ),
        out_specs=(P("section", "tensor", None), P("section", "tensor", None)),
        check_vma=False,
    )
```

profile of v0, /device:TPU:1, one launch (start us, length us, event | category | flops | bytes accessed | tf_op | source)
XLA Modules:
  0.0 192.3 jit_solution(17556186529246225966)
XLA Ops:
  7.2 3.8 %collective-permute-start = (bf16[8,8192]{1,0:T(8,128)(2,1)}, bf16[8,8192]{1,0:T(8,128)(2,1)S(1)}, u32[]{:S(2)}, u32[]{:S(2)}) collective-permute-start(bf16[8,8192]{1,0:T(8,128)(2,1)} %bitcast.29), channel_id=1, source_target_pairs={{0,1},{1,0},{2,3},{3,2},{4,5},{5,4},{6,7},{7,6},{8,9},{9,8},{10,11... | collective-permute-start | bytes 393224 | tf_op jit(solution)/shard_map/ppermute | solution.py:26
  17.7 4.0 %collective-permute-start.2 = (bf16[16,8192]{1,0:T(8,128)(2,1)S(1)}, bf16[16,8192]{1,0:T(8,128)(2,1)S(1)}, u32[]{:S(2)}, u32[]{:S(2)}) collective-permute-start(bf16[16,8192]{1,0:T(8,128)(2,1)S(1)} %fusion.2.refs_0_), channel_id=1, source_target_pairs={{0,14},{1,15},{2,0},{3,1},{4,2},{5,3},{6,4},{7,5},{8,6},{9,7},{10,... | collective-permute-start | bytes 786440 | tf_op jit(solution)/shard_map/ppermute | solution.py:20
  21.7 2.9 %collective-permute-start.1 = (bf16[16,8192]{1,0:T(8,128)(2,1)S(1)}, bf16[16,8192]{1,0:T(8,128)(2,1)S(1)}, u32[]{:S(2)}, u32[]{:S(2)}) collective-permute-start(bf16[16,8192]{1,0:T(8,128)(2,1)S(1)} %fusion.2.refs_0_), channel_id=1, source_target_pairs={{0,1},{1,0},{2,3},{3,2},{4,5},{5,4},{6,7},{7,6},{8,9},{9,8},{10,11... | collective-permute-start | bytes 786440 | tf_op jit(solution)/shard_map/ppermute | solution.py:26
  26.7 2.7 %collective-permute-start.7 = (bf16[16,8192]{1,0:T(8,128)(2,1)S(1)}, bf16[16,8192]{1,0:T(8,128)(2,1)S(1)}, u32[]{:S(2)}, u32[]{:S(2)}) collective-permute-start(bf16[16,8192]{1,0:T(8,128)(2,1)S(1)} %collective-permute-done.2.refs_2_), channel_id=1, source_target_pairs={{0,14},{1,15},{2,0},{3,1},{4,2},{5,3},{6,4},{7,5},{8,6},{9,7},{10,... | collective-permute-start | bytes 786440 | tf_op jit(solution)/shard_map/ppermute | solution.py:20
  29.4 2.9 %collective-permute-start.10 = (bf16[16,8192]{1,0:T(8,128)(2,1)S(1)}, bf16[16,8192]{1,0:T(8,128)(2,1)S(1)}, u32[]{:S(2)}, u32[]{:S(2)}) collective-permute-start(bf16[16,8192]{1,0:T(8,128)(2,1)S(1)} %collective-permute-done.3.refs_14_), channel_id=1, source_target_pairs={{0,1},{1,0},{2,3},{3,2},{4,5},{5,4},{6,7},{7,6},{8,9},{9,8},{10,11... | collective-permute-start | bytes 786440 | tf_op jit(solution)/shard_map/ppermute | solution.py:26
  33.5 2.9 %collective-permute-done.7.refs_4_ = bf16[16,8192]{1,0:T(8,128)(2,1)S(1)} collective-permute-done((bf16[16,8192]{1,0:T(8,128)(2,1)S(1)}, bf16[16,8192]{1,0:T(8,128)(2,1)S(1)}, u32[]{:S(2)}, u32[]{:S(2)}) %collective-permute-start.7) | collective-permute-done | bytes 262176 | tf_op jit(solution)/shard_map/ppermute | solution.py:20
  36.4 3.5 %collective-permute-start.8 = (bf16[16,8192]{1,0:T(8,128)(2,1)S(1)}, bf16[16,8192]{1,0:T(8,128)(2,1)S(1)}, u32[]{:S(2)}, u32[]{:S(2)}) collective-permute-start(bf16[16,8192]{1,0:T(8,128)(2,1)S(1)} %collective-permute-done.7.refs_4_), channel_id=1, source_target_pairs={{0,14},{1,15},{2,0},{3,1},{4,2},{5,3},{6,4},{7,5},{8,6},{9,7},{10,... | collective-permute-start | bytes 786440 | tf_op jit(solution)/shard_map/ppermute | solution.py:20
  39.9 2.9 %collective-permute-start.11 = (bf16[16,8192]{1,0:T(8,128)(2,1)S(1)}, bf16[16,8192]{1,0:T(8,128)(2,1)S(1)}, u32[]{:S(2)}, u32[]{:S(2)}) collective-permute-start(bf16[16,8192]{1,0:T(8,128)(2,1)S(1)} %collective-permute-done.7.refs_4_), channel_id=1, source_target_pairs={{0,1},{1,0},{2,3},{3,2},{4,5},{5,4},{6,7},{7,6},{8,9},{9,8},{10,11... | collective-permute-start | bytes 786440 | tf_op jit(solution)/shard_map/ppermute | solution.py:26
  42.9 4.3 %collective-permute-done.5.refs_10_ = bf16[16,8192]{1,0:T(8,128)(2,1)S(1)} collective-permute-done((bf16[16,8192]{1,0:T(8,128)(2,1)S(1)}, bf16[16,8192]{1,0:T(8,128)(2,1)S(1)}, u32[]{:S(2)}, u32[]{:S(2)}) %collective-permute-start.5) | collective-permute-done | bytes 262176 | tf_op jit(solution)/shard_map/ppermute | solution.py:20
  47.1 2.7 %collective-permute-done.8.refs_6_ = bf16[16,8192]{1,0:T(8,128)(2,1)S(1)} collective-permute-done((bf16[16,8192]{1,0:T(8,128)(2,1)S(1)}, bf16[16,8192]{1,0:T(8,128)(2,1)S(1)}, u32[]{:S(2)}, u32[]{:S(2)}) %collective-permute-start.8) | collective-permute-done | bytes 262176 | tf_op jit(solution)/shard_map/ppermute | solution.py:20
  49.9 3.5 %collective-permute-start.9 = (bf16[16,8192]{1,0:T(8,128)(2,1)S(1)}, bf16[16,8192]{1,0:T(8,128)(2,1)S(1)}, u32[]{:S(2)}, u32[]{:S(2)}) collective-permute-start(bf16[16,8192]{1,0:T(8,128)(2,1)S(1)} %collective-permute-done.1.refs_1_), channel_id=1, source_target_pairs={{0,14},{1,15},{2,0},{3,1},{4,2},{5,3},{6,4},{7,5},{8,6},{9,7},{10,... | collective-permute-start | bytes 786440 | tf_op jit(solution)/shard_map/ppermute | solution.py:20
  53.4 3.1 %collective-permute-start.12 = (bf16[16,8192]{1,0:T(8,128)(2,1)S(1)}, bf16[16,8192]{1,0:T(8,128)(2,1)S(1)}, u32[]{:S(2)}, u32[]{:S(2)}) collective-permute-start(bf16[16,8192]{1,0:T(8,128)(2,1)S(1)} %collective-permute-done.5.refs_10_), channel_id=1, source_target_pairs={{0,1},{1,0},{2,3},{3,2},{4,5},{5,4},{6,7},{7,6},{8,9},{9,8},{10,11... | collective-permute-start | bytes 786440 | tf_op jit(solution)/shard_map/ppermute | solution.py:26
  56.5 2.5 %collective-permute-start.13 = (bf16[128,512]{1,0:T(8,128)(2,1)}, bf16[128,512]{1,0:T(8,128)(2,1)S(1)}, u32[]{:S(2)}, u32[]{:S(2)}) collective-permute-start(bf16[128,512]{1,0:T(8,128)(2,1)} %bitcast.34), channel_id=1, source_target_pairs={{0,128},{16,144},{32,160},{48,176},{64,192},{80,208},{96,224},{112... | collective-permute-start | bytes 393224 | tf_op jit(solution)/shard_map/ppermute | solution.py:55
  62.8 3.5 %collective-permute-start.14 = (bf16[16,8192]{1,0:T(8,128)(2,1)S(1)}, bf16[16,8192]{1,0:T(8,128)(2,1)}, u32[]{:S(2)}, u32[]{:S(2)}) collective-permute-start(bf16[16,8192]{1,0:T(8,128)(2,1)S(1)} %collective-permute-done.11.refs_5_), channel_id=1, source_target_pairs={{0,14},{1,15},{2,0},{3,1},{4,2},{5,3},{6,4},{7,5},{8,6},{9,7},{10,... | collective-permute-start | bytes 786440 | tf_op jit(solution)/shard_map/ppermute | solution.py:20
  66.4 2.9 %collective-permute-start.15 = (bf16[16,8192]{1,0:T(8,128)(2,1)S(1)}, bf16[16,8192]{1,0:T(8,128)(2,1)}, u32[]{:S(2)}, u32[]{:S(2)}) collective-permute-start(bf16[16,8192]{1,0:T(8,128)(2,1)S(1)} %collective-permute-done.6.refs_8_), channel_id=1, source_target_pairs={{0,1},{1,0},{2,3},{3,2},{4,5},{5,4},{6,7},{7,6},{8,9},{9,8},{10,11... | collective-permute-start | bytes 786440 | tf_op jit(solution)/shard_map/ppermute | solution.py:26
  73.0 4.9 %shard_map.113 = (bf16[128,256]{1,0:T(8,128)(2,1)S(1)}, bf16[128,128]{1,0:T(8,128)(2,1)S(1)}, bf16[128,128]{1,0:T(8,128)(2,1)S(1)}) custom-call(s32[1]{0:T(128)} %bitcast.where, bf16[128,8192]{1,0:T(8,128)(2,1)S(1)} %copy-done.4, bf16[256,8192]{1,0:T(8,128)(2,1)S(1)} %bitcast.25, bf16[128,512]{1,0:T(8,128)(2,1)S(1)} %collective-permute-done.13.saved, ...), custom_call_target="tpu_custom_call" | custom-call | flops 536870912 | bytes 6291456 | tf_op jit(solution)/shard_map/pallas_call | solution.py:345
  79.8 2.7 %collective-permute-start.19 = (bf16[8,8192]{1,0:T(8,128)(2,1)}, bf16[8,8192]{1,0:T(8,128)(2,1)}, u32[]{:S(2)}, u32[]{:S(2)}) collective-permute-start(bf16[8,8192]{1,0:T(8,128)(2,1)} %bitcast.13), channel_id=1, source_target_pairs={{0,128},{16,144},{32,160},{48,176},{64,192},{80,208},{96,224},{112... | collective-permute-start | bytes 393224 | tf_op jit(solution)/shard_map/ppermute | solution.py:356
  82.5 5.3 %shard_map.114 = (bf16[256,256]{1,0:T(8,128)(2,1)S(1)}, bf16[256,128]{1,0:T(8,128)(2,1)}) custom-call(bf16[16,8192]{1,0:T(8,128)(2,1)S(1)} %fusion.2.refs_0_, bf16[16,8192]{1,0:T(8,128)(2,1)S(1)} %collective-permute-done.1.refs_1_, bf16[16,8192]{1,0:T(8,128)(2,1)S(1)} %collective-permute-done.2.refs_2_, bf16[16,8192]{1,0:T(8,128)(2,1)S(1)} %collective-permute-done.9.refs_3_, ...), custom_call_target="tpu_custom_call" | custom-call | flops 1610612736 | bytes 10485760 | tf_op jit(solution)/shard_map/pallas_call | solution.py:358
  89.4 4.4 %shard_map.115 = bf16[128,8192]{1,0:T(8,128)(2,1)} custom-call(bf16[128,256]{1,0:T(8,128)(2,1)S(1)} %get-tuple-element.114.grad_q, bf16[128,128]{1,0:T(8,128)(2,1)S(1)} %get-tuple-element.115.own, bf16[128,128]{1,0:T(8,128)(2,1)S(1)} %collective-permute-done.18.partner, bf16[8192,256]{1,0:T(8,128)(2,1)S(1)} %bitcast.24, bf16[128,8192]{1,0:T(8,128)(2,1)S(1)} %bitcast.28), custom_call_target="tpu_custom_call" | custom-call | flops 805306368 | bytes 8388608 | tf_op jit(solution)/shard_map/pallas_call | solution.py:369
  96.1 5.8 %shard_map.116 = (bf16[16,8192]{1,0:T(8,128)(2,1)S(1)}, bf16[16,8192]{1,0:T(8,128)(2,1)S(1)}, bf16[16,8192]{1,0:T(8,128)(2,1)S(1)}, bf16[16,8192]{1,0:T(8,128)(2...) custom-call(s32[1]{0:T(128)} %bitcast.where, ...), custom_call_target="tpu_custom_call" | custom-call | flops 1073741824 | bytes 8388608 | tf_op jit(solution)/shard_map/pallas_call | solution.py:382
  107.6 2.5 %collective-permute-done.20 = bf16[16,8192]{1,0:T(8,128)(2,1)} collective-permute-done((bf16[16,8192]{1,0:T(8,128)(2,1)}, bf16[16,8192]{1,0:T(8,128)(2,1)}, u32[]{:S(2)}, u32[]{:S(2)}) %collective-permute-start.20) | collective-permute-done | bytes 262176 | tf_op jit(solution)/shard_map/ppermute | solution.py:20
  116.8 2.8 %collective-permute-done.21 = bf16[16,8192]{1,0:T(8,128)(2,1)S(1)} collective-permute-done((bf16[16,8192]{1,0:T(8,128)(2,1)S(1)}, bf16[16,8192]{1,0:T(8,128)(2,1)S(1)}, u32[]{:S(2)}, u32[]{:S(2)}) %collective-permute-start.21) | collective-permute-done | bytes 262176 | tf_op jit(solution)/shard_map/ppermute | solution.py:20
  122.2 3.6 %collective-permute-start.30 = (bf16[16,8192]{1,0:T(8,128)(2,1)S(1)}, bf16[16,8192]{1,0:T(8,128)(2,1)S(1)}, u32[]{:S(2)}, u32[]{:S(2)}) collective-permute-start(bf16[16,8192]{1,0:T(8,128)(2,1)S(1)} %add_convert_fusion.5), channel_id=1, source_target_pairs={{0,14},{1,15},{2,0},{3,1},{4,2},{5,3},{6,4},{7,5},{8,6},{9,7},{10,... | collective-permute-start | bytes 786440 | tf_op jit(solution)/shard_map/ppermute | solution.py:20
  125.8 7.3 %collective-permute-done.32 = bf16[16,8192]{1,0:T(8,128)(2,1)S(1)} collective-permute-done((bf16[16,8192]{1,0:T(8,128)(2,1)S(1)}, bf16[16,8192]{1,0:T(8,128)(2,1)S(1)}, u32[]{:S(2)}, u32[]{:S(2)}) %collective-permute-start.32) | collective-permute-done | bytes 262176 | tf_op jit(solution)/shard_map/ppermute | solution.py:20
  133.4 2.8 %collective-permute-done.30 = bf16[16,8192]{1,0:T(8,128)(2,1)S(1)} collective-permute-done((bf16[16,8192]{1,0:T(8,128)(2,1)S(1)}, bf16[16,8192]{1,0:T(8,128)(2,1)S(1)}, u32[]{:S(2)}, u32[]{:S(2)}) %collective-permute-start.30) | collective-permute-done | bytes 262176 | tf_op jit(solution)/shard_map/ppermute | solution.py:20
  136.3 3.6 %collective-permute-start.31 = (bf16[16,8192]{1,0:T(8,128)(2,1)S(1)}, bf16[16,8192]{1,0:T(8,128)(2,1)S(1)}, u32[]{:S(2)}, u32[]{:S(2)}) collective-permute-start(bf16[16,8192]{1,0:T(8,128)(2,1)S(1)} %add_convert_fusion.4), channel_id=1, source_target_pairs={{0,14},{1,15},{2,0},{3,1},{4,2},{5,3},{6,4},{7,5},{8,6},{9,7},{10,... | collective-permute-start | bytes 786440 | tf_op jit(solution)/shard_map/ppermute | solution.py:20
  139.9 6.3 %collective-permute-done.33 = bf16[16,8192]{1,0:T(8,128)(2,1)S(1)} collective-permute-done((bf16[16,8192]{1,0:T(8,128)(2,1)S(1)}, bf16[16,8192]{1,0:T(8,128)(2,1)S(1)}, u32[]{:S(2)}, u32[]{:S(2)}) %collective-permute-start.33) | collective-permute-done | bytes 262176 | tf_op jit(solution)/shard_map/ppermute | solution.py:20
  148.2 8.6 %reduce-scatter.2.cloned.1.call-done = bf16[16,8192]{1,0:T(8,128)(2,1)} async-done(((bf16[128,8192]{1,0:T(8,128)(2,1)}), bf16[16,8192]{1,0:T(8,128)(2,1)}) %reduce-scatter.2.cloned.1.call-update) | async-done | bytes 262160 | tf_op jit(solution)/shard_map/reduce_scatter | solution.py:378
  160.1 6.3 %collective-permute-start.27 = (bf16[16,8192]{1,0:T(8,128)(2,1)S(1)}, bf16[16,8192]{1,0:T(8,128)(2,1)S(1)}, u32[]{:S(2)}, u32[]{:S(2)}) collective-permute-start(bf16[16,8192]{1,0:T(8,128)(2,1)S(1)} %add_convert_fusion.9), channel_id=1, source_target_pairs={{0,17},{1,16},{2,19},{3,18},{4,21},{5,20},{6,23},{7,22},{8,25},{9,... | collective-permute-start | bytes 786440 | tf_op jit(solution)/shard_map/ppermute | solution.py:83
  168.3 4.0 %collective-permute-start.34 = (bf16[16,8192]{1,0:T(8,128)(2,1)S(1)}, bf16[16,8192]{1,0:T(8,128)(2,1)S(1)}, u32[]{:S(2)}, u32[]{:S(2)}) collective-permute-start(bf16[16,8192]{1,0:T(8,128)(2,1)S(1)} %add_convert_fusion.3), channel_id=1, source_target_pairs={{0,30},{1,31},{2,16},{3,17},{4,18},{5,19},{6,20},{7,21},{8,22},{9,... | collective-permute-start | bytes 786440 | tf_op jit(solution)/shard_map/ppermute | solution.py:83
  176.9 4.4 %collective-permute-done.37 = bf16[8,8192]{1,0:T(8,128)(2,1)S(1)} collective-permute-done((bf16[8,8192]{1,0:T(8,128)(2,1)S(1)}, bf16[8,8192]{1,0:T(8,128)(2,1)S(1)}, u32[]{:S(2)}, u32[]{:S(2)}) %collective-permute-start.37) | collective-permute-done | bytes 131104 | tf_op jit(solution)/shard_map/ppermute | solution.py:407
  181.3 2.7 %collective-permute-done.35 = bf16[16,8192]{1,0:T(8,128)(2,1)S(1)} collective-permute-done((bf16[16,8192]{1,0:T(8,128)(2,1)S(1)}, bf16[16,8192]{1,0:T(8,128)(2,1)S(1)}, u32[]{:S(2)}, u32[]{:S(2)}) %collective-permute-start.35) | collective-permute-done | bytes 262176 | tf_op jit(solution)/shard_map/ppermute | solution.py:83
  (103 shorter events, 51.9 us)
Async XLA Ops:
  7.2 62.1 %all-gather.2.cloned.1.call-start = ((), (), s32[]{:S(2)}) async-start(), calls=%async_computation.1 | async-start | bytes 2359296 | tf_op jit(solution)/shard_map/all_gather | solution.py:342
  15.3 141.5 %reduce-scatter.2.cloned.1.call-start = ((), (), s32[]{:S(2)}) async-start(), calls=%async_computation.2 | async-start | bytes 2359296 | tf_op jit(solution)/shard_map/reduce_scatter | solution.py:378
  15.4 11.3 %collective-permute-start.3 = (bf16[16,8192]{1,0:T(8,128)(2,1)S(1)}, bf16[16,8192]{1,0:T(8,128)(2,1)S(1)}, u32[]{:S(2)}, u32[]{:S(2)}) collective-permute-start(bf16[16,8192]{1,0:T(8,128)(2,1)S(1)} %fusion.2.refs_0_), channel_id=1, source_target_pairs={{0,2},{1,3},{2,4},{3,5},{4,6},{5,7},{6,8},{7,9},{8,10},{9,11},{10,... | collective-permute-start | bytes 786440 | tf_op jit(solution)/shard_map/ppermute | solution.py:20
  17.7 9.0 %collective-permute-start.2 = (bf16[16,8192]{1,0:T(8,128)(2,1)S(1)}, bf16[16,8192]{1,0:T(8,128)(2,1)S(1)}, u32[]{:S(2)}, u32[]{:S(2)}) collective-permute-start(bf16[16,8192]{1,0:T(8,128)(2,1)S(1)} %fusion.2.refs_0_), channel_id=1, source_target_pairs={{0,14},{1,15},{2,0},{3,1},{4,2},{5,3},{6,4},{7,5},{8,6},{9,7},{10,... | collective-permute-start | bytes 786440 | tf_op jit(solution)/shard_map/ppermute | solution.py:20
  26.7 9.7 %collective-permute-start.7 = (bf16[16,8192]{1,0:T(8,128)(2,1)S(1)}, bf16[16,8192]{1,0:T(8,128)(2,1)S(1)}, u32[]{:S(2)}, u32[]{:S(2)}) collective-permute-start(bf16[16,8192]{1,0:T(8,128)(2,1)S(1)} %collective-permute-done.2.refs_2_), channel_id=1, source_target_pairs={{0,14},{1,15},{2,0},{3,1},{4,2},{5,3},{6,4},{7,5},{8,6},{9,7},{10,... | collective-permute-start | bytes 786440 | tf_op jit(solution)/shard_map/ppermute | solution.py:20
  29.4 10.5 %collective-permute-start.10 = (bf16[16,8192]{1,0:T(8,128)(2,1)S(1)}, bf16[16,8192]{1,0:T(8,128)(2,1)S(1)}, u32[]{:S(2)}, u32[]{:S(2)}) collective-permute-start(bf16[16,8192]{1,0:T(8,128)(2,1)S(1)} %collective-permute-done.3.refs_14_), channel_id=1, source_target_pairs={{0,1},{1,0},{2,3},{3,2},{4,5},{5,4},{6,7},{7,6},{8,9},{9,8},{10,11... | collective-permute-start | bytes 786440 | tf_op jit(solution)/shard_map/ppermute | solution.py:26
  33.5 13.6 %collective-permute-start.5 = (bf16[16,8192]{1,0:T(8,128)(2,1)S(1)}, bf16[16,8192]{1,0:T(8,128)(2,1)S(1)}, u32[]{:S(2)}, u32[]{:S(2)}) collective-permute-start(bf16[16,8192]{1,0:T(8,128)(2,1)S(1)} %collective-permute-done.4.refs_12_), channel_id=1, source_target_pairs={{0,2},{1,3},{2,4},{3,5},{4,6},{5,7},{6,8},{7,9},{8,10},{9,11},{10,... | collective-permute-start | bytes 786440 | tf_op jit(solution)/shard_map/ppermute | solution.py:20
  36.4 13.5 %collective-permute-start.8 = (bf16[16,8192]{1,0:T(8,128)(2,1)S(1)}, bf16[16,8192]{1,0:T(8,128)(2,1)S(1)}, u32[]{:S(2)}, u32[]{:S(2)}) collective-permute-start(bf16[16,8192]{1,0:T(8,128)(2,1)S(1)} %collective-permute-done.7.refs_4_), channel_id=1, source_target_pairs={{0,14},{1,15},{2,0},{3,1},{4,2},{5,3},{6,4},{7,5},{8,6},{9,7},{10,... | collective-permute-start | bytes 786440 | tf_op jit(solution)/shard_map/ppermute | solution.py:20
  39.9 13.5 %collective-permute-start.11 = (bf16[16,8192]{1,0:T(8,128)(2,1)S(1)}, bf16[16,8192]{1,0:T(8,128)(2,1)S(1)}, u32[]{:S(2)}, u32[]{:S(2)}) collective-permute-start(bf16[16,8192]{1,0:T(8,128)(2,1)S(1)} %collective-permute-done.7.refs_4_), channel_id=1, source_target_pairs={{0,1},{1,0},{2,3},{3,2},{4,5},{5,4},{6,7},{7,6},{8,9},{9,8},{10,11... | collective-permute-start | bytes 786440 | tf_op jit(solution)/shard_map/ppermute | solution.py:26
  47.1 13.3 %collective-permute-start.6 = (bf16[16,8192]{1,0:T(8,128)(2,1)S(1)}, bf16[16,8192]{1,0:T(8,128)(2,1)S(1)}, u32[]{:S(2)}, u32[]{:S(2)}) collective-permute-start(bf16[16,8192]{1,0:T(8,128)(2,1)S(1)} %collective-permute-done.5.refs_10_), channel_id=1, source_target_pairs={{0,2},{1,3},{2,4},{3,5},{4,6},{5,7},{6,8},{7,9},{8,10},{9,11},{10,... | collective-permute-start | bytes 786440 | tf_op jit(solution)/shard_map/ppermute | solution.py:20
  49.9 13.0 %collective-permute-start.9 = (bf16[16,8192]{1,0:T(8,128)(2,1)S(1)}, bf16[16,8192]{1,0:T(8,128)(2,1)S(1)}, u32[]{:S(2)}, u32[]{:S(2)}) collective-permute-start(bf16[16,8192]{1,0:T(8,128)(2,1)S(1)} %collective-permute-done.1.refs_1_), channel_id=1, source_target_pairs={{0,14},{1,15},{2,0},{3,1},{4,2},{5,3},{6,4},{7,5},{8,6},{9,7},{10,... | collective-permute-start | bytes 786440 | tf_op jit(solution)/shard_map/ppermute | solution.py:20
  53.4 13.0 %collective-permute-start.12 = (bf16[16,8192]{1,0:T(8,128)(2,1)S(1)}, bf16[16,8192]{1,0:T(8,128)(2,1)S(1)}, u32[]{:S(2)}, u32[]{:S(2)}) collective-permute-start(bf16[16,8192]{1,0:T(8,128)(2,1)S(1)} %collective-permute-done.5.refs_10_), channel_id=1, source_target_pairs={{0,1},{1,0},{2,3},{3,2},{4,5},{5,4},{6,7},{7,6},{8,9},{9,8},{10,11... | collective-permute-start | bytes 786440 | tf_op jit(solution)/shard_map/ppermute | solution.py:26
  56.5 9.9 %collective-permute-start.13 = (bf16[128,512]{1,0:T(8,128)(2,1)}, bf16[128,512]{1,0:T(8,128)(2,1)S(1)}, u32[]{:S(2)}, u32[]{:S(2)}) collective-permute-start(bf16[128,512]{1,0:T(8,128)(2,1)} %bitcast.34), channel_id=1, source_target_pairs={{0,128},{16,144},{32,160},{48,176},{64,192},{80,208},{96,224},{112... | collective-permute-start | bytes 393224 | tf_op jit(solution)/shard_map/ppermute | solution.py:55
  60.4 17.5 %collective-permute-start.16 = (bf16[16,8192]{1,0:T(8,128)(2,1)S(1)}, bf16[16,8192]{1,0:T(8,128)(2,1)}, u32[]{:S(2)}, u32[]{:S(2)}) collective-permute-start(bf16[16,8192]{1,0:T(8,128)(2,1)S(1)} %collective-permute-done.10.refs_15_), channel_id=1, source_target_pairs={{0,2},{1,3},{2,4},{3,5},{4,6},{5,7},{6,8},{7,9},{8,10},{9,11},{10,... | collective-permute-start | bytes 786440 | tf_op jit(solution)/shard_map/ppermute | solution.py:20
  62.8 15.1 %collective-permute-start.14 = (bf16[16,8192]{1,0:T(8,128)(2,1)S(1)}, bf16[16,8192]{1,0:T(8,128)(2,1)}, u32[]{:S(2)}, u32[]{:S(2)}) collective-permute-start(bf16[16,8192]{1,0:T(8,128)(2,1)S(1)} %collective-permute-done.11.refs_5_), channel_id=1, source_target_pairs={{0,14},{1,15},{2,0},{3,1},{4,2},{5,3},{6,4},{7,5},{8,6},{9,7},{10,... | collective-permute-start | bytes 786440 | tf_op jit(solution)/shard_map/ppermute | solution.py:20
  66.4 11.6 %collective-permute-start.15 = (bf16[16,8192]{1,0:T(8,128)(2,1)S(1)}, bf16[16,8192]{1,0:T(8,128)(2,1)}, u32[]{:S(2)}, u32[]{:S(2)}) collective-permute-start(bf16[16,8192]{1,0:T(8,128)(2,1)S(1)} %collective-permute-done.6.refs_8_), channel_id=1, source_target_pairs={{0,1},{1,0},{2,3},{3,2},{4,5},{5,4},{6,7},{7,6},{8,9},{9,8},{10,11... | collective-permute-start | bytes 786440 | tf_op jit(solution)/shard_map/ppermute | solution.py:26
  78.0 11.5 %collective-permute-start.18 = (bf16[128,128]{1,0:T(8,128)(2,1)S(1)}, bf16[128,128]{1,0:T(8,128)(2,1)S(1)}, u32[]{:S(2)}, u32[]{:S(2)}) collective-permute-start(bf16[128,128]{1,0:T(8,128)(2,1)S(1)} %get-tuple-element.116), channel_id=1, source_target_pairs={{0,1},{1,0},{2,3},{3,2},{4,5},{5,4},{6,7},{7,6},{8,9},{9,8},{10,11... | collective-permute-start | bytes 98312 | tf_op jit(solution)/shard_map/ppermute | solution.py:26
  79.8 14.1 %collective-permute-start.19 = (bf16[8,8192]{1,0:T(8,128)(2,1)}, bf16[8,8192]{1,0:T(8,128)(2,1)}, u32[]{:S(2)}, u32[]{:S(2)}) collective-permute-start(bf16[8,8192]{1,0:T(8,128)(2,1)} %bitcast.13), channel_id=1, source_target_pairs={{0,128},{16,144},{32,160},{48,176},{64,192},{80,208},{96,224},{112... | collective-permute-start | bytes 393224 | tf_op jit(solution)/shard_map/ppermute | solution.py:356
  110.0 9.5 %collective-permute-start.21 = (bf16[16,8192]{1,0:T(8,128)(2,1)S(1)}, bf16[16,8192]{1,0:T(8,128)(2,1)S(1)}, u32[]{:S(2)}, u32[]{:S(2)}) collective-permute-start(bf16[16,8192]{1,0:T(8,128)(2,1)S(1)} %copy-done.8), channel_id=1, source_target_pairs={{0,2},{1,3},{2,4},{3,5},{4,6},{5,7},{6,8},{7,9},{8,10},{9,11},{10,... | collective-permute-start | bytes 786440 | tf_op jit(solution)/shard_map/ppermute | solution.py:20
  111.7 7.9 %collective-permute-start.24 = (bf16[16,8192]{1,0:T(8,128)(2,1)S(1)}, bf16[16,8192]{1,0:T(8,128)(2,1)S(1)}, u32[]{:S(2)}, u32[]{:S(2)}) collective-permute-start(bf16[16,8192]{1,0:T(8,128)(2,1)S(1)} %get-tuple-element.128), channel_id=1, source_target_pairs={{0,1},{1,0},{2,3},{3,2},{4,5},{5,4},{6,7},{7,6},{8,9},{9,8},{10,11... | collective-permute-start | bytes 786440 | tf_op jit(solution)/shard_map/ppermute | solution.py:26
  113.4 8.6 %collective-permute-start.29 = (bf16[16,8192]{1,0:T(8,128)(2,1)S(1)}, bf16[16,8192]{1,0:T(8,128)(2,1)S(1)}, u32[]{:S(2)}, u32[]{:S(2)}) collective-permute-start(bf16[16,8192]{1,0:T(8,128)(2,1)S(1)} %add_convert_fusion.6), channel_id=1, source_target_pairs={{0,14},{1,15},{2,0},{3,1},{4,2},{5,3},{6,4},{7,5},{8,6},{9,7},{10,... | collective-permute-start | bytes 786440 | tf_op jit(solution)/shard_map/ppermute | solution.py:20
  119.5 13.6 %collective-permute-start.32 = (bf16[16,8192]{1,0:T(8,128)(2,1)S(1)}, bf16[16,8192]{1,0:T(8,128)(2,1)S(1)}, u32[]{:S(2)}, u32[]{:S(2)}) collective-permute-start(bf16[16,8192]{1,0:T(8,128)(2,1)S(1)} %get-tuple-element.145), channel_id=1, source_target_pairs={{0,2},{1,3},{2,4},{3,5},{4,6},{5,7},{6,8},{7,9},{8,10},{9,11},{10,... | collective-permute-start | bytes 786440 | tf_op jit(solution)/shard_map/ppermute | solution.py:20
  119.7 13.4 %collective-permute-start.25 = (bf16[16,8192]{1,0:T(8,128)(2,1)S(1)}, bf16[16,8192]{1,0:T(8,128)(2,1)S(1)}, u32[]{:S(2)}, u32[]{:S(2)}) collective-permute-start(bf16[16,8192]{1,0:T(8,128)(2,1)S(1)} %add_convert_fusion.7), channel_id=1, source_target_pairs={{0,1},{1,0},{2,3},{3,2},{4,5},{5,4},{6,7},{7,6},{8,9},{9,8},{10,11... | collective-permute-start | bytes 786440 | tf_op jit(solution)/shard_map/ppermute | solution.py:26
  122.2 14.0 %collective-permute-start.30 = (bf16[16,8192]{1,0:T(8,128)(2,1)S(1)}, bf16[16,8192]{1,0:T(8,128)(2,1)S(1)}, u32[]{:S(2)}, u32[]{:S(2)}) collective-permute-start(bf16[16,8192]{1,0:T(8,128)(2,1)S(1)} %add_convert_fusion.5), channel_id=1, source_target_pairs={{0,14},{1,15},{2,0},{3,1},{4,2},{5,3},{6,4},{7,5},{8,6},{9,7},{10,... | collective-permute-start | bytes 786440 | tf_op jit(solution)/shard_map/ppermute | solution.py:20
  133.2 13.1 %collective-permute-start.26 = (bf16[16,8192]{1,0:T(8,128)(2,1)S(1)}, bf16[16,8192]{1,0:T(8,128)(2,1)S(1)}, u32[]{:S(2)}, u32[]{:S(2)}) collective-permute-start(bf16[16,8192]{1,0:T(8,128)(2,1)S(1)} %add_convert_fusion.8), channel_id=1, source_target_pairs={{0,1},{1,0},{2,3},{3,2},{4,5},{5,4},{6,7},{7,6},{8,9},{9,8},{10,11... | collective-permute-start | bytes 786440 | tf_op jit(solution)/shard_map/ppermute | solution.py:26
  133.3 12.9 %collective-permute-start.33 = (bf16[16,8192]{1,0:T(8,128)(2,1)S(1)}, bf16[16,8192]{1,0:T(8,128)(2,1)S(1)}, u32[]{:S(2)}, u32[]{:S(2)}) collective-permute-start(bf16[16,8192]{1,0:T(8,128)(2,1)S(1)} %add_convert_fusion.2), channel_id=1, source_target_pairs={{0,2},{1,3},{2,4},{3,5},{4,6},{5,7},{6,8},{7,9},{8,10},{9,11},{10,... | collective-permute-start | bytes 786440 | tf_op jit(solution)/shard_map/ppermute | solution.py:20
  136.3 11.8 %collective-permute-start.31 = (bf16[16,8192]{1,0:T(8,128)(2,1)S(1)}, bf16[16,8192]{1,0:T(8,128)(2,1)S(1)}, u32[]{:S(2)}, u32[]{:S(2)}) collective-permute-start(bf16[16,8192]{1,0:T(8,128)(2,1)S(1)} %add_convert_fusion.4), channel_id=1, source_target_pairs={{0,14},{1,15},{2,0},{3,1},{4,2},{5,3},{6,4},{7,5},{8,6},{9,7},{10,... | collective-permute-start | bytes 786440 | tf_op jit(solution)/shard_map/ppermute | solution.py:20
  157.8 16.5 %collective-permute-start.36 = (bf16[8,8192]{1,0:T(8,128)(2,1)S(1)}, bf16[8,8192]{1,0:T(8,128)(2,1)S(1)}, u32[]{:S(2)}, u32[]{:S(2)}) collective-permute-start(bf16[8,8192]{1,0:T(8,128)(2,1)S(1)} %broadcast_select_fusion), channel_id=1, source_target_pairs={{0,1},{1,0},{2,3},{3,2},{4,5},{5,4},{6,7},{7,6},{8,9},{9,8},{10,11... | collective-permute-start | bytes 393224 | tf_op jit(solution)/shard_map/ppermute | solution.py:26
  160.1 21.2 %collective-permute-start.27 = (bf16[16,8192]{1,0:T(8,128)(2,1)S(1)}, bf16[16,8192]{1,0:T(8,128)(2,1)S(1)}, u32[]{:S(2)}, u32[]{:S(2)}) collective-permute-start(bf16[16,8192]{1,0:T(8,128)(2,1)S(1)} %add_convert_fusion.9), channel_id=1, source_target_pairs={{0,17},{1,16},{2,19},{3,18},{4,21},{5,20},{6,23},{7,22},{8,25},{9,... | collective-permute-start | bytes 786440 | tf_op jit(solution)/shard_map/ppermute | solution.py:83
  166.3 14.9 %collective-permute-start.28 = (bf16[16,8192]{1,0:T(8,128)(2,1)S(1)}, bf16[16,8192]{1,0:T(8,128)(2,1)S(1)}, u32[]{:S(2)}, u32[]{:S(2)}) collective-permute-start(bf16[16,8192]{1,0:T(8,128)(2,1)S(1)} %fusion.3), channel_id=1, source_target_pairs={{0,16},{1,17},{2,18},{3,19},{4,20},{5,21},{6,22},{7,23},{8,24},{9,... | collective-permute-start | bytes 786440 | tf_op jit(solution)/shard_map/ppermute | solution.py:83
  168.3 13.0 %collective-permute-start.34 = (bf16[16,8192]{1,0:T(8,128)(2,1)S(1)}, bf16[16,8192]{1,0:T(8,128)(2,1)S(1)}, u32[]{:S(2)}, u32[]{:S(2)}) collective-permute-start(bf16[16,8192]{1,0:T(8,128)(2,1)S(1)} %add_convert_fusion.3), channel_id=1, source_target_pairs={{0,30},{1,31},{2,16},{3,17},{4,18},{5,19},{6,20},{7,21},{8,22},{9,... | collective-permute-start | bytes 786440 | tf_op jit(solution)/shard_map/ppermute | solution.py:83
  172.3 11.7 %collective-permute-start.35 = (bf16[16,8192]{1,0:T(8,128)(2,1)S(1)}, bf16[16,8192]{1,0:T(8,128)(2,1)S(1)}, u32[]{:S(2)}, u32[]{:S(2)}) collective-permute-start(bf16[16,8192]{1,0:T(8,128)(2,1)S(1)} %add_convert_fusion.1), channel_id=1, source_target_pairs={{0,18},{1,19},{2,20},{3,21},{4,22},{5,23},{6,24},{7,25},{8,26},{9,... | collective-permute-start | bytes 786440 | tf_op jit(solution)/shard_map/ppermute | solution.py:83
  (22 other events, 275.2 us)
Sparse Core Ops, SparseCore 0:
  15.4 53.0 all-gather.1
  105.4 51.3 reduce-scatter.1
where the time goes:
time: 193 us; the launch traced here: 192 us
  starting transfers between devices  79.2 us (41%)
  waiting for transfers between devices  58.5 us (30%)
  Pallas kernels  20.4 us (11%)
  between operations  14.4 us (7%)
  other arithmetic  11.8 us (6%)
  local copies, waits for them, and re-layouts  8.04 us (4%)
    ppermute x18, waiting for transfers between devices, along_z(): lax.ppermute(x, 'tensor', [(t, (t // 2 + k) % RING * 2 + t % 2) for t in...  41.6 us
    ppermute x18, starting transfers between devices, along_z(): lax.ppermute(x, 'tensor', [(t, (t // 2 + k) % RING * 2 + t % 2) for t in...  31.7 us
    ppermute x13, starting transfers between devices, across(): return lax.ppermute(x, 'tensor', [(t, t ^ 1) for t in range(2 * RING)])  27.9 us
    ppermute x4, starting transfers between devices, onward(): return lax.ppermute(x, ('section', 'tensor'), pairs)  14.2 us
    reduce_scatter x1, waiting for transfers between devices, local(): lax.psum_scatter(term, 'tensor', scatter_dimension=0, tiled=True, axis_in...  8.56 us
    unnamed x29, local copies, waits for them, and re-layouts  8.04 us
    pallas_call x1, Pallas kernels, local(): call(attend_kernel, 2 * fwd_tokens * features * width, 2 * features * (wi...  5.79 us
    pallas_call x1, Pallas kernels, local(): call(project_kernel, 2 * fwd_tokens * features * (width + HD), 2 * featur...  5.34 us
  transfers between devices with their start and end apart: 40, of which 20 were waited for; matrix products, arithmetic and copies ran while one was open for 4% of the time, Pallas kernels for 8%

commit v1 on v0

--- a/solution.py
+++ b/solution.py
@@ -98,14 +98,13 @@
     from_up, from_down, from_side = down(a[5]), up(a[3]), side(b[2])
     a[6] = add_blocks(a[6], from_up)
     a[2] = add_blocks(a[2], from_down, from_side)
-    from_up, from_down, from_side = down(a[6]), up(a[2]), side(b[7])
+    from_up, from_down = down(a[6]), up(a[2])
+    from_side = side(b[7])
+    first = [onward(after(b[0], from_side), 0, 1), onward(after(a[0], from_side), 0, 0)]
     a[7] = add_blocks(a[7], from_up, from_side)
     a[1] = add_blocks(a[1], from_down)
-    last = [onward(after(b[0], from_side), 0, 1)]
-    last += [onward(after(a[0], from_side), 0, 0)]
     a[7], a[1], beside = lax.optimization_barrier((a[7], a[1], beside))
-    last += [onward(a[7], -1, 0), onward(a[1], 1, 0)]
-    return last, beside
+    return first + [onward(a[7], -1, 0), onward(a[1], 1, 0)], beside
 
 
 def norm_rows(inputs, gain_vector):
@@ -305,6 +304,10 @@
     return pl.BlockSpec(memory_space=pltpu.HBM)
 
 
+def in_hbm(x):
+    return pltpu.with_memory_space_constraint(x, pltpu.HBM)
+
+
 def scalars():
     return pl.BlockSpec(memory_space=pltpu.SMEM)
 
@@ -350,7 +353,7 @@
         [scalars(), far(), far(), held(), held()],
         [held()] * 3,
         [(bwd_tokens, features), (width, features)],
-    )(where_now, grads_all, out_weight, saved_block, bwd_segments)
+    )(where_now, in_hbm(grads_all), in_hbm(out_weight), saved_block, bwd_segments)
     pieces, other_half = lax.optimization_barrier((pieces, other_half))
     partner_half = across(other_half)
     saved_rows = lax.ppermute(after(parked_input[0], other_half), "section", mirror)
@@ -394,7 +397,7 @@
         own_kv,
         after(other_kv, term, saved_rows),
         fwd_segments,
-        out_weight,
+        in_hbm(out_weight),
     )
     fwd_parts, pair_sums = scatter_relative(pair_sums, shares, residual)
 

time: 193 us -> 190 us (0.984)
  local copies, waits for them, and re-layouts: 8.04 us -> 2.08 us
  starting transfers between devices: 79.2 us -> 82 us
    unnamed x29 -> x23, local copies, waits for them, and re-layouts: 8.04 us -> 2.08 us
    reduce_scatter x1, waiting for transfers between devices: 8.56 us -> 4.01 us  [local(): lax.psum_scatter(term, 'tensor', scatter_dimension=0, tiled=True, axis_in...]
    ppermute x18, waiting for transfers between devices: 41.6 us -> 45.3 us  [along_z(): lax.ppermute(x, 'tensor', [(t, (t // 2 + k) % RING * 2 + t % 2) for t in...]
    ppermute x4, starting transfers between devices: 14.2 us -> 16.9 us  [onward(): return lax.ppermute(x, ('section', 'tensor'), pairs)]
where the time goes in v1:
time: 190 us; the launch traced here: 189 us
  starting transfers between devices  82 us (43%)
  waiting for transfers between devices  57.6 us (30%)
  Pallas kernels  21.5 us (11%)
  between operations  14.4 us (8%)
  other arithmetic  11.8 us (6%)
  local copies, waits for them, and re-layouts  2.08 us (1%)
    ppermute x18, waiting for transfers between devices, along_z(): lax.ppermute(x, 'tensor', [(t, (t // 2 + k) % RING * 2 + t % 2) for t in...  45.3 us
    ppermute x18, starting transfers between devices, along_z(): lax.ppermute(x, 'tensor', [(t, (t // 2 + k) % RING * 2 + t % 2) for t in...  32.2 us
    ppermute x13, starting transfers between devices, across(): return lax.ppermute(x, 'tensor', [(t, t ^ 1) for t in range(2 * RING)])  27.6 us
    ppermute x4, starting transfers between devices, onward(): return lax.ppermute(x, ('section', 'tensor'), pairs)  16.9 us
    pallas_call x1, Pallas kernels, local(): call(attend_kernel, 2 * fwd_tokens * features * width, 2 * features * (wi...  5.92 us
    pallas_call x1, Pallas kernels, local(): call(backward_kernel, 2 * bwd_tokens * features * width, 2 * features * (...  5.87 us
    pallas_call x1, Pallas kernels, local(): call(project_kernel, 2 * fwd_tokens * features * (width + HD), 2 * featur...  5.34 us
    pallas_call x1, Pallas kernels, local(): call(term_kernel, 2 * bwd_tokens * features * (width + HD), 2 * features...  4.4 us
  transfers between devices with their start and end apart: 40, of which 20 were waited for; matrix products, arithmetic and copies ran while one was open for 4% of the time, Pallas kernels for 8%

profile of v1, /device:TPU:1, one launch (start us, length us, event | category | flops | bytes accessed | tf_op | source)
XLA Modules:
  0.0 189.4 jit_solution(12229507756284128773)
XLA Ops:
  7.2 3.8 %collective-permute-start = (bf16[8,8192]{1,0:T(8,128)(2,1)}, bf16[8,8192]{1,0:T(8,128)(2,1)S(1)}, u32[]{:S(2)}, u32[]{:S(2)}) collective-permute-start(bf16[8,8192]{1,0:T(8,128)(2,1)} %bitcast.29), channel_id=1, source_target_pairs={{0,1},{1,0},{2,3},{3,2},{4,5},{5,4},{6,7},{7,6},{8,9},{9,8},{10,11... | collective-permute-start | bytes 393224 | tf_op jit(solution)/shard_map/ppermute | solution.py:26
  17.7 4.0 %collective-permute-start.2 = (bf16[16,8192]{1,0:T(8,128)(2,1)S(1)}, bf16[16,8192]{1,0:T(8,128)(2,1)S(1)}, u32[]{:S(2)}, u32[]{:S(2)}) collective-permute-start(bf16[16,8192]{1,0:T(8,128)(2,1)S(1)} %fusion.2.refs_0_), channel_id=1, source_target_pairs={{0,14},{1,15},{2,0},{3,1},{4,2},{5,3},{6,4},{7,5},{8,6},{9,7},{10,... | collective-permute-start | bytes 786440 | tf_op jit(solution)/shard_map/ppermute | solution.py:20
  21.7 2.9 %collective-permute-start.1 = (bf16[16,8192]{1,0:T(8,128)(2,1)S(1)}, bf16[16,8192]{1,0:T(8,128)(2,1)S(1)}, u32[]{:S(2)}, u32[]{:S(2)}) collective-permute-start(bf16[16,8192]{1,0:T(8,128)(2,1)S(1)} %fusion.2.refs_0_), channel_id=1, source_target_pairs={{0,1},{1,0},{2,3},{3,2},{4,5},{5,4},{6,7},{7,6},{8,9},{9,8},{10,11... | collective-permute-start | bytes 786440 | tf_op jit(solution)/shard_map/ppermute | solution.py:26
  26.7 2.7 %collective-permute-start.7 = (bf16[16,8192]{1,0:T(8,128)(2,1)S(1)}, bf16[16,8192]{1,0:T(8,128)(2,1)S(1)}, u32[]{:S(2)}, u32[]{:S(2)}) collective-permute-start(bf16[16,8192]{1,0:T(8,128)(2,1)S(1)} %collective-permute-done.2.refs_2_), channel_id=1, source_target_pairs={{0,14},{1,15},{2,0},{3,1},{4,2},{5,3},{6,4},{7,5},{8,6},{9,7},{10,... | collective-permute-start | bytes 786440 | tf_op jit(solution)/shard_map/ppermute | solution.py:20
  29.4 2.9 %collective-permute-start.10 = (bf16[16,8192]{1,0:T(8,128)(2,1)S(1)}, bf16[16,8192]{1,0:T(8,128)(2,1)S(1)}, u32[]{:S(2)}, u32[]{:S(2)}) collective-permute-start(bf16[16,8192]{1,0:T(8,128)(2,1)S(1)} %collective-permute-done.3.refs_14_), channel_id=1, source_target_pairs={{0,1},{1,0},{2,3},{3,2},{4,5},{5,4},{6,7},{7,6},{8,9},{9,8},{10,11... | collective-permute-start | bytes 786440 | tf_op jit(solution)/shard_map/ppermute | solution.py:26
  33.5 2.9 %collective-permute-done.7.refs_4_ = bf16[16,8192]{1,0:T(8,128)(2,1)S(1)} collective-permute-done((bf16[16,8192]{1,0:T(8,128)(2,1)S(1)}, bf16[16,8192]{1,0:T(8,128)(2,1)S(1)}, u32[]{:S(2)}, u32[]{:S(2)}) %collective-permute-start.7) | collective-permute-done | bytes 262176 | tf_op jit(solution)/shard_map/ppermute | solution.py:20
  36.4 3.5 %collective-permute-start.8 = (bf16[16,8192]{1,0:T(8,128)(2,1)S(1)}, bf16[16,8192]{1,0:T(8,128)(2,1)S(1)}, u32[]{:S(2)}, u32[]{:S(2)}) collective-permute-start(bf16[16,8192]{1,0:T(8,128)(2,1)S(1)} %collective-permute-done.7.refs_4_), channel_id=1, source_target_pairs={{0,14},{1,15},{2,0},{3,1},{4,2},{5,3},{6,4},{7,5},{8,6},{9,7},{10,... | collective-permute-start | bytes 786440 | tf_op jit(solution)/shard_map/ppermute | solution.py:20
  39.9 2.9 %collective-permute-start.11 = (bf16[16,8192]{1,0:T(8,128)(2,1)S(1)}, bf16[16,8192]{1,0:T(8,128)(2,1)S(1)}, u32[]{:S(2)}, u32[]{:S(2)}) collective-permute-start(bf16[16,8192]{1,0:T(8,128)(2,1)S(1)} %collective-permute-done.7.refs_4_), channel_id=1, source_target_pairs={{0,1},{1,0},{2,3},{3,2},{4,5},{5,4},{6,7},{7,6},{8,9},{9,8},{10,11... | collective-permute-start | bytes 786440 | tf_op jit(solution)/shard_map/ppermute | solution.py:26
  42.9 4.3 %collective-permute-done.5.refs_10_ = bf16[16,8192]{1,0:T(8,128)(2,1)S(1)} collective-permute-done((bf16[16,8192]{1,0:T(8,128)(2,1)S(1)}, bf16[16,8192]{1,0:T(8,128)(2,1)S(1)}, u32[]{:S(2)}, u32[]{:S(2)}) %collective-permute-start.5) | collective-permute-done | bytes 262176 | tf_op jit(solution)/shard_map/ppermute | solution.py:20
  47.1 2.7 %collective-permute-done.8.refs_6_ = bf16[16,8192]{1,0:T(8,128)(2,1)S(1)} collective-permute-done((bf16[16,8192]{1,0:T(8,128)(2,1)S(1)}, bf16[16,8192]{1,0:T(8,128)(2,1)S(1)}, u32[]{:S(2)}, u32[]{:S(2)}) %collective-permute-start.8) | collective-permute-done | bytes 262176 | tf_op jit(solution)/shard_map/ppermute | solution.py:20
  49.9 3.5 %collective-permute-start.9 = (bf16[16,8192]{1,0:T(8,128)(2,1)S(1)}, bf16[16,8192]{1,0:T(8,128)(2,1)S(1)}, u32[]{:S(2)}, u32[]{:S(2)}) collective-permute-start(bf16[16,8192]{1,0:T(8,128)(2,1)S(1)} %collective-permute-done.1.refs_1_), channel_id=1, source_target_pairs={{0,14},{1,15},{2,0},{3,1},{4,2},{5,3},{6,4},{7,5},{8,6},{9,7},{10,... | collective-permute-start | bytes 786440 | tf_op jit(solution)/shard_map/ppermute | solution.py:20
  53.4 3.1 %collective-permute-start.12 = (bf16[16,8192]{1,0:T(8,128)(2,1)S(1)}, bf16[16,8192]{1,0:T(8,128)(2,1)S(1)}, u32[]{:S(2)}, u32[]{:S(2)}) collective-permute-start(bf16[16,8192]{1,0:T(8,128)(2,1)S(1)} %collective-permute-done.5.refs_10_), channel_id=1, source_target_pairs={{0,1},{1,0},{2,3},{3,2},{4,5},{5,4},{6,7},{7,6},{8,9},{9,8},{10,11... | collective-permute-start | bytes 786440 | tf_op jit(solution)/shard_map/ppermute | solution.py:26
  56.5 2.5 %collective-permute-start.13 = (bf16[128,512]{1,0:T(8,128)(2,1)}, bf16[128,512]{1,0:T(8,128)(2,1)S(1)}, u32[]{:S(2)}, u32[]{:S(2)}) collective-permute-start(bf16[128,512]{1,0:T(8,128)(2,1)} %bitcast.34), channel_id=1, source_target_pairs={{0,128},{16,144},{32,160},{48,176},{64,192},{80,208},{96,224},{112... | collective-permute-start | bytes 393224 | tf_op jit(solution)/shard_map/ppermute | solution.py:55
  62.8 3.5 %collective-permute-start.14 = (bf16[16,8192]{1,0:T(8,128)(2,1)S(1)}, bf16[16,8192]{1,0:T(8,128)(2,1)}, u32[]{:S(2)}, u32[]{:S(2)}) collective-permute-start(bf16[16,8192]{1,0:T(8,128)(2,1)S(1)} %collective-permute-done.11.refs_5_), channel_id=1, source_target_pairs={{0,14},{1,15},{2,0},{3,1},{4,2},{5,3},{6,4},{7,5},{8,6},{9,7},{10,... | collective-permute-start | bytes 786440 | tf_op jit(solution)/shard_map/ppermute | solution.py:20
  66.4 2.9 %collective-permute-start.15 = (bf16[16,8192]{1,0:T(8,128)(2,1)S(1)}, bf16[16,8192]{1,0:T(8,128)(2,1)}, u32[]{:S(2)}, u32[]{:S(2)}) collective-permute-start(bf16[16,8192]{1,0:T(8,128)(2,1)S(1)} %collective-permute-done.6.refs_8_), channel_id=1, source_target_pairs={{0,1},{1,0},{2,3},{3,2},{4,5},{5,4},{6,7},{7,6},{8,9},{9,8},{10,11... | collective-permute-start | bytes 786440 | tf_op jit(solution)/shard_map/ppermute | solution.py:26
  69.3 5.9 %shard_map.113 = (bf16[128,256]{1,0:T(8,128)(2,1)S(1)}, bf16[128,128]{1,0:T(8,128)(2,1)S(1)}, bf16[128,128]{1,0:T(8,128)(2,1)S(1)}) custom-call(s32[1]{0:T(128)} %bitcast.where, bf16[128,8192]{1,0:T(8,128)(2,1)} %all-gather.2.cloned.1.call-done.grads, bf16[256,8192]{1,0:T(8,128)(2,1)} %bitcast.27, bf16[128,512]{1,0:T(8,128)(2,1)S(1)} %collective-permute-done.13.saved, ...), custom_call_target="tpu_custom_call" | custom-call | flops 536870912 | bytes 6291456 | tf_op jit(solution)/shard_map/pallas_call | solution.py:348
  77.0 2.7 %collective-permute-start.19 = (bf16[8,8192]{1,0:T(8,128)(2,1)}, bf16[8,8192]{1,0:T(8,128)(2,1)}, u32[]{:S(2)}, u32[]{:S(2)}) collective-permute-start(bf16[8,8192]{1,0:T(8,128)(2,1)} %bitcast.13), channel_id=1, source_target_pairs={{0,128},{16,144},{32,160},{48,176},{64,192},{80,208},{96,224},{112... | collective-permute-start | bytes 393224 | tf_op jit(solution)/shard_map/ppermute | solution.py:359
  79.7 5.3 %shard_map.114 = (bf16[256,256]{1,0:T(8,128)(2,1)S(1)}, bf16[256,128]{1,0:T(8,128)(2,1)}) custom-call(bf16[16,8192]{1,0:T(8,128)(2,1)S(1)} %fusion.2.refs_0_, bf16[16,8192]{1,0:T(8,128)(2,1)S(1)} %collective-permute-done.1.refs_1_, bf16[16,8192]{1,0:T(8,128)(2,1)S(1)} %collective-permute-done.2.refs_2_, bf16[16,8192]{1,0:T(8,128)(2,1)S(1)} %collective-permute-done.9.refs_3_, ...), custom_call_target="tpu_custom_call" | custom-call | flops 1610612736 | bytes 10485760 | tf_op jit(solution)/shard_map/pallas_call | solution.py:361
  86.6 4.4 %shard_map.115 = bf16[128,8192]{1,0:T(8,128)(2,1)} custom-call(bf16[128,256]{1,0:T(8,128)(2,1)S(1)} %get-tuple-element.114.grad_q, bf16[128,128]{1,0:T(8,128)(2,1)S(1)} %get-tuple-element.115.own, bf16[128,128]{1,0:T(8,128)(2,1)S(1)} %collective-permute-done.18.partner, bf16[8192,256]{1,0:T(8,128)(2,1)S(1)} %bitcast.24, bf16[128,8192]{1,0:T(8,128)(2,1)S(1)} %bitcast.26), custom_call_target="tpu_custom_call" | custom-call | flops 805306368 | bytes 8388608 | tf_op jit(solution)/shard_map/pallas_call | solution.py:372
  91.1 5.9 %shard_map.116 = (bf16[16,8192]{1,0:T(8,128)(2,1)S(1)}, bf16[16,8192]{1,0:T(8,128)(2,1)S(1)}, bf16[16,8192]{1,0:T(8,128)(2,1)S(1)}, bf16[16,8192]{1,0:T(8,128)(2...) custom-call(s32[1]{0:T(128)} %bitcast.where, ...), custom_call_target="tpu_custom_call" | custom-call | flops 1073741824 | bytes 8388608 | tf_op jit(solution)/shard_map/pallas_call | solution.py:385
  100.4 2.5 %collective-permute-start.22 = (bf16[16,8192]{1,0:T(8,128)(2,1)}, bf16[16,8192]{1,0:T(8,128)(2,1)S(1)}, u32[]{:S(2)}, u32[]{:S(2)}) collective-permute-start(bf16[16,8192]{1,0:T(8,128)(2,1)} %copy-done.6), channel_id=1, source_target_pairs={{0,14},{1,15},{2,0},{3,1},{4,2},{5,3},{6,4},{7,5},{8,6},{9,7},{10,... | collective-permute-start | bytes 786440 | tf_op jit(solution)/shard_map/ppermute | solution.py:20
  108.6 2.5 %collective-permute-start.29 = (bf16[16,8192]{1,0:T(8,128)(2,1)S(1)}, bf16[16,8192]{1,0:T(8,128)(2,1)S(1)}, u32[]{:S(2)}, u32[]{:S(2)}) collective-permute-start(bf16[16,8192]{1,0:T(8,128)(2,1)S(1)} %add_convert_fusion.6), channel_id=1, source_target_pairs={{0,14},{1,15},{2,0},{3,1},{4,2},{5,3},{6,4},{7,5},{8,6},{9,7},{10,... | collective-permute-start | bytes 786440 | tf_op jit(solution)/shard_map/ppermute | solution.py:20
  118.9 3.6 %collective-permute-start.30 = (bf16[16,8192]{1,0:T(8,128)(2,1)S(1)}, bf16[16,8192]{1,0:T(8,128)(2,1)S(1)}, u32[]{:S(2)}, u32[]{:S(2)}) collective-permute-start(bf16[16,8192]{1,0:T(8,128)(2,1)S(1)} %add_convert_fusion.5), channel_id=1, source_target_pairs={{0,14},{1,15},{2,0},{3,1},{4,2},{5,3},{6,4},{7,5},{8,6},{9,7},{10,... | collective-permute-start | bytes 786440 | tf_op jit(solution)/shard_map/ppermute | solution.py:20
  122.5 4.7 %collective-permute-done.32 = bf16[16,8192]{1,0:T(8,128)(2,1)S(1)} collective-permute-done((bf16[16,8192]{1,0:T(8,128)(2,1)S(1)}, bf16[16,8192]{1,0:T(8,128)(2,1)S(1)}, u32[]{:S(2)}, u32[]{:S(2)}) %collective-permute-start.32) | collective-permute-done | bytes 262176 | tf_op jit(solution)/shard_map/ppermute | solution.py:20
  127.5 6.1 %collective-permute-done.30 = bf16[16,8192]{1,0:T(8,128)(2,1)S(1)} collective-permute-done((bf16[16,8192]{1,0:T(8,128)(2,1)S(1)}, bf16[16,8192]{1,0:T(8,128)(2,1)S(1)}, u32[]{:S(2)}, u32[]{:S(2)}) %collective-permute-start.30) | collective-permute-done | bytes 262176 | tf_op jit(solution)/shard_map/ppermute | solution.py:20
  133.7 3.6 %collective-permute-start.31 = (bf16[16,8192]{1,0:T(8,128)(2,1)S(1)}, bf16[16,8192]{1,0:T(8,128)(2,1)S(1)}, u32[]{:S(2)}, u32[]{:S(2)}) collective-permute-start(bf16[16,8192]{1,0:T(8,128)(2,1)S(1)} %add_convert_fusion.4), channel_id=1, source_target_pairs={{0,14},{1,15},{2,0},{3,1},{4,2},{5,3},{6,4},{7,5},{8,6},{9,7},{10,... | collective-permute-start | bytes 786440 | tf_op jit(solution)/shard_map/ppermute | solution.py:20
  137.3 2.6 %collective-permute-done.33 = bf16[16,8192]{1,0:T(8,128)(2,1)S(1)} collective-permute-done((bf16[16,8192]{1,0:T(8,128)(2,1)S(1)}, bf16[16,8192]{1,0:T(8,128)(2,1)S(1)}, u32[]{:S(2)}, u32[]{:S(2)}) %collective-permute-start.33) | collective-permute-done | bytes 262176 | tf_op jit(solution)/shard_map/ppermute | solution.py:20
  140.0 8.4 %collective-permute-done.31 = bf16[16,8192]{1,0:T(8,128)(2,1)S(1)} collective-permute-done((bf16[16,8192]{1,0:T(8,128)(2,1)S(1)}, bf16[16,8192]{1,0:T(8,128)(2,1)S(1)}, u32[]{:S(2)}, u32[]{:S(2)}) %collective-permute-start.31) | collective-permute-done | bytes 262176 | tf_op jit(solution)/shard_map/ppermute | solution.py:20
  148.5 4.0 %reduce-scatter.2.cloned.1.call-done = bf16[16,8192]{1,0:T(8,128)(2,1)} async-done(((bf16[128,8192]{1,0:T(8,128)(2,1)}), bf16[16,8192]{1,0:T(8,128)(2,1)}) %reduce-scatter.2.cloned.1.call-update) | async-done | bytes 262160 | tf_op jit(solution)/shard_map/reduce_scatter | solution.py:381
  155.0 7.3 %collective-permute-start.27 = (bf16[16,8192]{1,0:T(8,128)(2,1)S(1)}, bf16[16,8192]{1,0:T(8,128)(2,1)S(1)}, u32[]{:S(2)}, u32[]{:S(2)}) collective-permute-start(bf16[16,8192]{1,0:T(8,128)(2,1)S(1)} %add_convert_fusion.9), channel_id=1, source_target_pairs={{0,17},{1,16},{2,19},{3,18},{4,21},{5,20},{6,23},{7,22},{8,25},{9,... | collective-permute-start | bytes 786440 | tf_op jit(solution)/shard_map/ppermute | solution.py:83
  164.2 5.8 %collective-permute-start.34 = (bf16[16,8192]{1,0:T(8,128)(2,1)S(1)}, bf16[16,8192]{1,0:T(8,128)(2,1)S(1)}, u32[]{:S(2)}, u32[]{:S(2)}) collective-permute-start(bf16[16,8192]{1,0:T(8,128)(2,1)S(1)} %add_convert_fusion.3), channel_id=1, source_target_pairs={{0,30},{1,31},{2,16},{3,17},{4,18},{5,19},{6,20},{7,21},{8,22},{9,... | collective-permute-start | bytes 786440 | tf_op jit(solution)/shard_map/ppermute | solution.py:83
  174.5 4.4 %collective-permute-done.37 = bf16[8,8192]{1,0:T(8,128)(2,1)S(1)} collective-permute-done((bf16[8,8192]{1,0:T(8,128)(2,1)S(1)}, bf16[8,8192]{1,0:T(8,128)(2,1)S(1)}, u32[]{:S(2)}, u32[]{:S(2)}) %collective-permute-start.37) | collective-permute-done | bytes 131104 | tf_op jit(solution)/shard_map/ppermute | solution.py:410
  (97 shorter events, 47.3 us)
Async XLA Ops:
  7.2 62.1 %all-gather.2.cloned.1.call-start = ((), (), s32[]{:S(2)}) async-start(), calls=%async_computation.1 | async-start | bytes 2359296 | tf_op jit(solution)/shard_map/all_gather | solution.py:345
  15.3 137.2 %reduce-scatter.2.cloned.1.call-start = ((), (), s32[]{:S(2)}) async-start(), calls=%async_computation.2 | async-start | bytes 2359296 | tf_op jit(solution)/shard_map/reduce_scatter | solution.py:381
  15.4 11.3 %collective-permute-start.3 = (bf16[16,8192]{1,0:T(8,128)(2,1)S(1)}, bf16[16,8192]{1,0:T(8,128)(2,1)S(1)}, u32[]{:S(2)}, u32[]{:S(2)}) collective-permute-start(bf16[16,8192]{1,0:T(8,128)(2,1)S(1)} %fusion.2.refs_0_), channel_id=1, source_target_pairs={{0,2},{1,3},{2,4},{3,5},{4,6},{5,7},{6,8},{7,9},{8,10},{9,11},{10,... | collective-permute-start | bytes 786440 | tf_op jit(solution)/shard_map/ppermute | solution.py:20
  17.7 9.0 %collective-permute-start.2 = (bf16[16,8192]{1,0:T(8,128)(2,1)S(1)}, bf16[16,8192]{1,0:T(8,128)(2,1)S(1)}, u32[]{:S(2)}, u32[]{:S(2)}) collective-permute-start(bf16[16,8192]{1,0:T(8,128)(2,1)S(1)} %fusion.2.refs_0_), channel_id=1, source_target_pairs={{0,14},{1,15},{2,0},{3,1},{4,2},{5,3},{6,4},{7,5},{8,6},{9,7},{10,... | collective-permute-start | bytes 786440 | tf_op jit(solution)/shard_map/ppermute | solution.py:20
  26.7 9.7 %collective-permute-start.7 = (bf16[16,8192]{1,0:T(8,128)(2,1)S(1)}, bf16[16,8192]{1,0:T(8,128)(2,1)S(1)}, u32[]{:S(2)}, u32[]{:S(2)}) collective-permute-start(bf16[16,8192]{1,0:T(8,128)(2,1)S(1)} %collective-permute-done.2.refs_2_), channel_id=1, source_target_pairs={{0,14},{1,15},{2,0},{3,1},{4,2},{5,3},{6,4},{7,5},{8,6},{9,7},{10,... | collective-permute-start | bytes 786440 | tf_op jit(solution)/shard_map/ppermute | solution.py:20
  29.4 10.5 %collective-permute-start.10 = (bf16[16,8192]{1,0:T(8,128)(2,1)S(1)}, bf16[16,8192]{1,0:T(8,128)(2,1)S(1)}, u32[]{:S(2)}, u32[]{:S(2)}) collective-permute-start(bf16[16,8192]{1,0:T(8,128)(2,1)S(1)} %collective-permute-done.3.refs_14_), channel_id=1, source_target_pairs={{0,1},{1,0},{2,3},{3,2},{4,5},{5,4},{6,7},{7,6},{8,9},{9,8},{10,11... | collective-permute-start | bytes 786440 | tf_op jit(solution)/shard_map/ppermute | solution.py:26
  33.5 13.6 %collective-permute-start.5 = (bf16[16,8192]{1,0:T(8,128)(2,1)S(1)}, bf16[16,8192]{1,0:T(8,128)(2,1)S(1)}, u32[]{:S(2)}, u32[]{:S(2)}) collective-permute-start(bf16[16,8192]{1,0:T(8,128)(2,1)S(1)} %collective-permute-done.4.refs_12_), channel_id=1, source_target_pairs={{0,2},{1,3},{2,4},{3,5},{4,6},{5,7},{6,8},{7,9},{8,10},{9,11},{10,... | collective-permute-start | bytes 786440 | tf_op jit(solution)/shard_map/ppermute | solution.py:20
  36.4 13.5 %collective-permute-start.8 = (bf16[16,8192]{1,0:T(8,128)(2,1)S(1)}, bf16[16,8192]{1,0:T(8,128)(2,1)S(1)}, u32[]{:S(2)}, u32[]{:S(2)}) collective-permute-start(bf16[16,8192]{1,0:T(8,128)(2,1)S(1)} %collective-permute-done.7.refs_4_), channel_id=1, source_target_pairs={{0,14},{1,15},{2,0},{3,1},{4,2},{5,3},{6,4},{7,5},{8,6},{9,7},{10,... | collective-permute-start | bytes 786440 | tf_op jit(solution)/shard_map/ppermute | solution.py:20
  39.9 13.5 %collective-permute-start.11 = (bf16[16,8192]{1,0:T(8,128)(2,1)S(1)}, bf16[16,8192]{1,0:T(8,128)(2,1)S(1)}, u32[]{:S(2)}, u32[]{:S(2)}) collective-permute-start(bf16[16,8192]{1,0:T(8,128)(2,1)S(1)} %collective-permute-done.7.refs_4_), channel_id=1, source_target_pairs={{0,1},{1,0},{2,3},{3,2},{4,5},{5,4},{6,7},{7,6},{8,9},{9,8},{10,11... | collective-permute-start | bytes 786440 | tf_op jit(solution)/shard_map/ppermute | solution.py:26
  47.1 13.3 %collective-permute-start.6 = (bf16[16,8192]{1,0:T(8,128)(2,1)S(1)}, bf16[16,8192]{1,0:T(8,128)(2,1)S(1)}, u32[]{:S(2)}, u32[]{:S(2)}) collective-permute-start(bf16[16,8192]{1,0:T(8,128)(2,1)S(1)} %collective-permute-done.5.refs_10_), channel_id=1, source_target_pairs={{0,2},{1,3},{2,4},{3,5},{4,6},{5,7},{6,8},{7,9},{8,10},{9,11},{10,... | collective-permute-start | bytes 786440 | tf_op jit(solution)/shard_map/ppermute | solution.py:20
  49.9 13.0 %collective-permute-start.9 = (bf16[16,8192]{1,0:T(8,128)(2,1)S(1)}, bf16[16,8192]{1,0:T(8,128)(2,1)S(1)}, u32[]{:S(2)}, u32[]{:S(2)}) collective-permute-start(bf16[16,8192]{1,0:T(8,128)(2,1)S(1)} %collective-permute-done.1.refs_1_), channel_id=1, source_target_pairs={{0,14},{1,15},{2,0},{3,1},{4,2},{5,3},{6,4},{7,5},{8,6},{9,7},{10,... | collective-permute-start | bytes 786440 | tf_op jit(solution)/shard_map/ppermute | solution.py:20
  53.4 13.0 %collective-permute-start.12 = (bf16[16,8192]{1,0:T(8,128)(2,1)S(1)}, bf16[16,8192]{1,0:T(8,128)(2,1)S(1)}, u32[]{:S(2)}, u32[]{:S(2)}) collective-permute-start(bf16[16,8192]{1,0:T(8,128)(2,1)S(1)} %collective-permute-done.5.refs_10_), channel_id=1, source_target_pairs={{0,1},{1,0},{2,3},{3,2},{4,5},{5,4},{6,7},{7,6},{8,9},{9,8},{10,11... | collective-permute-start | bytes 786440 | tf_op jit(solution)/shard_map/ppermute | solution.py:26
  56.5 9.9 %collective-permute-start.13 = (bf16[128,512]{1,0:T(8,128)(2,1)}, bf16[128,512]{1,0:T(8,128)(2,1)S(1)}, u32[]{:S(2)}, u32[]{:S(2)}) collective-permute-start(bf16[128,512]{1,0:T(8,128)(2,1)} %bitcast.34), channel_id=1, source_target_pairs={{0,128},{16,144},{32,160},{48,176},{64,192},{80,208},{96,224},{112... | collective-permute-start | bytes 393224 | tf_op jit(solution)/shard_map/ppermute | solution.py:55
  60.4 14.7 %collective-permute-start.16 = (bf16[16,8192]{1,0:T(8,128)(2,1)S(1)}, bf16[16,8192]{1,0:T(8,128)(2,1)}, u32[]{:S(2)}, u32[]{:S(2)}) collective-permute-start(bf16[16,8192]{1,0:T(8,128)(2,1)S(1)} %collective-permute-done.10.refs_15_), channel_id=1, source_target_pairs={{0,2},{1,3},{2,4},{3,5},{4,6},{5,7},{6,8},{7,9},{8,10},{9,11},{10,... | collective-permute-start | bytes 786440 | tf_op jit(solution)/shard_map/ppermute | solution.py:20
  62.8 12.3 %collective-permute-start.14 = (bf16[16,8192]{1,0:T(8,128)(2,1)S(1)}, bf16[16,8192]{1,0:T(8,128)(2,1)}, u32[]{:S(2)}, u32[]{:S(2)}) collective-permute-start(bf16[16,8192]{1,0:T(8,128)(2,1)S(1)} %collective-permute-done.11.refs_5_), channel_id=1, source_target_pairs={{0,14},{1,15},{2,0},{3,1},{4,2},{5,3},{6,4},{7,5},{8,6},{9,7},{10,... | collective-permute-start | bytes 786440 | tf_op jit(solution)/shard_map/ppermute | solution.py:20
  66.4 8.8 %collective-permute-start.15 = (bf16[16,8192]{1,0:T(8,128)(2,1)S(1)}, bf16[16,8192]{1,0:T(8,128)(2,1)}, u32[]{:S(2)}, u32[]{:S(2)}) collective-permute-start(bf16[16,8192]{1,0:T(8,128)(2,1)S(1)} %collective-permute-done.6.refs_8_), channel_id=1, source_target_pairs={{0,1},{1,0},{2,3},{3,2},{4,5},{5,4},{6,7},{7,6},{8,9},{9,8},{10,11... | collective-permute-start | bytes 786440 | tf_op jit(solution)/shard_map/ppermute | solution.py:26
  75.2 11.5 %collective-permute-start.18 = (bf16[128,128]{1,0:T(8,128)(2,1)S(1)}, bf16[128,128]{1,0:T(8,128)(2,1)S(1)}, u32[]{:S(2)}, u32[]{:S(2)}) collective-permute-start(bf16[128,128]{1,0:T(8,128)(2,1)S(1)} %get-tuple-element.116), channel_id=1, source_target_pairs={{0,1},{1,0},{2,3},{3,2},{4,5},{5,4},{6,7},{7,6},{8,9},{9,8},{10,11... | collective-permute-start | bytes 98312 | tf_op jit(solution)/shard_map/ppermute | solution.py:26
  77.0 14.1 %collective-permute-start.19 = (bf16[8,8192]{1,0:T(8,128)(2,1)}, bf16[8,8192]{1,0:T(8,128)(2,1)}, u32[]{:S(2)}, u32[]{:S(2)}) collective-permute-start(bf16[8,8192]{1,0:T(8,128)(2,1)} %bitcast.13), channel_id=1, source_target_pairs={{0,128},{16,144},{32,160},{48,176},{64,192},{80,208},{96,224},{112... | collective-permute-start | bytes 393224 | tf_op jit(solution)/shard_map/ppermute | solution.py:359
  105.2 9.3 %collective-permute-start.21 = (bf16[16,8192]{1,0:T(8,128)(2,1)S(1)}, bf16[16,8192]{1,0:T(8,128)(2,1)S(1)}, u32[]{:S(2)}, u32[]{:S(2)}) collective-permute-start(bf16[16,8192]{1,0:T(8,128)(2,1)S(1)} %copy-done.5), channel_id=1, source_target_pairs={{0,2},{1,3},{2,4},{3,5},{4,6},{5,7},{6,8},{7,9},{8,10},{9,11},{10,... | collective-permute-start | bytes 786440 | tf_op jit(solution)/shard_map/ppermute | solution.py:20
  106.9 8.3 %collective-permute-start.24 = (bf16[16,8192]{1,0:T(8,128)(2,1)S(1)}, bf16[16,8192]{1,0:T(8,128)(2,1)S(1)}, u32[]{:S(2)}, u32[]{:S(2)}) collective-permute-start(bf16[16,8192]{1,0:T(8,128)(2,1)S(1)} %get-tuple-element.128), channel_id=1, source_target_pairs={{0,1},{1,0},{2,3},{3,2},{4,5},{5,4},{6,7},{7,6},{8,9},{9,8},{10,11... | collective-permute-start | bytes 786440 | tf_op jit(solution)/shard_map/ppermute | solution.py:26
  108.6 10.1 %collective-permute-start.29 = (bf16[16,8192]{1,0:T(8,128)(2,1)S(1)}, bf16[16,8192]{1,0:T(8,128)(2,1)S(1)}, u32[]{:S(2)}, u32[]{:S(2)}) collective-permute-start(bf16[16,8192]{1,0:T(8,128)(2,1)S(1)} %add_convert_fusion.6), channel_id=1, source_target_pairs={{0,14},{1,15},{2,0},{3,1},{4,2},{5,3},{6,4},{7,5},{8,6},{9,7},{10,... | collective-permute-start | bytes 786440 | tf_op jit(solution)/shard_map/ppermute | solution.py:20
  114.4 12.8 %collective-permute-start.32 = (bf16[16,8192]{1,0:T(8,128)(2,1)S(1)}, bf16[16,8192]{1,0:T(8,128)(2,1)S(1)}, u32[]{:S(2)}, u32[]{:S(2)}) collective-permute-start(bf16[16,8192]{1,0:T(8,128)(2,1)S(1)} %get-tuple-element.145), channel_id=1, source_target_pairs={{0,2},{1,3},{2,4},{3,5},{4,6},{5,7},{6,8},{7,9},{8,10},{9,11},{10,... | collective-permute-start | bytes 786440 | tf_op jit(solution)/shard_map/ppermute | solution.py:20
  115.1 12.1 %collective-permute-start.25 = (bf16[16,8192]{1,0:T(8,128)(2,1)S(1)}, bf16[16,8192]{1,0:T(8,128)(2,1)S(1)}, u32[]{:S(2)}, u32[]{:S(2)}) collective-permute-start(bf16[16,8192]{1,0:T(8,128)(2,1)S(1)} %add_convert_fusion.7), channel_id=1, source_target_pairs={{0,1},{1,0},{2,3},{3,2},{4,5},{5,4},{6,7},{7,6},{8,9},{9,8},{10,11... | collective-permute-start | bytes 786440 | tf_op jit(solution)/shard_map/ppermute | solution.py:26
  118.9 14.7 %collective-permute-start.30 = (bf16[16,8192]{1,0:T(8,128)(2,1)S(1)}, bf16[16,8192]{1,0:T(8,128)(2,1)S(1)}, u32[]{:S(2)}, u32[]{:S(2)}) collective-permute-start(bf16[16,8192]{1,0:T(8,128)(2,1)S(1)} %add_convert_fusion.5), channel_id=1, source_target_pairs={{0,14},{1,15},{2,0},{3,1},{4,2},{5,3},{6,4},{7,5},{8,6},{9,7},{10,... | collective-permute-start | bytes 786440 | tf_op jit(solution)/shard_map/ppermute | solution.py:20
  127.3 12.6 %collective-permute-start.26 = (bf16[16,8192]{1,0:T(8,128)(2,1)S(1)}, bf16[16,8192]{1,0:T(8,128)(2,1)S(1)}, u32[]{:S(2)}, u32[]{:S(2)}) collective-permute-start(bf16[16,8192]{1,0:T(8,128)(2,1)S(1)} %add_convert_fusion.8), channel_id=1, source_target_pairs={{0,1},{1,0},{2,3},{3,2},{4,5},{5,4},{6,7},{7,6},{8,9},{9,8},{10,11... | collective-permute-start | bytes 786440 | tf_op jit(solution)/shard_map/ppermute | solution.py:26
  127.4 12.5 %collective-permute-start.33 = (bf16[16,8192]{1,0:T(8,128)(2,1)S(1)}, bf16[16,8192]{1,0:T(8,128)(2,1)S(1)}, u32[]{:S(2)}, u32[]{:S(2)}) collective-permute-start(bf16[16,8192]{1,0:T(8,128)(2,1)S(1)} %add_convert_fusion.2), channel_id=1, source_target_pairs={{0,2},{1,3},{2,4},{3,5},{4,6},{5,7},{6,8},{7,9},{8,10},{9,11},{10,... | collective-permute-start | bytes 786440 | tf_op jit(solution)/shard_map/ppermute | solution.py:20
  133.7 14.6 %collective-permute-start.31 = (bf16[16,8192]{1,0:T(8,128)(2,1)S(1)}, bf16[16,8192]{1,0:T(8,128)(2,1)S(1)}, u32[]{:S(2)}, u32[]{:S(2)}) collective-permute-start(bf16[16,8192]{1,0:T(8,128)(2,1)S(1)} %add_convert_fusion.4), channel_id=1, source_target_pairs={{0,14},{1,15},{2,0},{3,1},{4,2},{5,3},{6,4},{7,5},{8,6},{9,7},{10,... | collective-permute-start | bytes 786440 | tf_op jit(solution)/shard_map/ppermute | solution.py:20
  153.5 18.5 %collective-permute-start.36 = (bf16[8,8192]{1,0:T(8,128)(2,1)S(1)}, bf16[8,8192]{1,0:T(8,128)(2,1)S(1)}, u32[]{:S(2)}, u32[]{:S(2)}) collective-permute-start(bf16[8,8192]{1,0:T(8,128)(2,1)S(1)} %broadcast_select_fusion), channel_id=1, source_target_pairs={{0,1},{1,0},{2,3},{3,2},{4,5},{5,4},{6,7},{7,6},{8,9},{9,8},{10,11... | collective-permute-start | bytes 393224 | tf_op jit(solution)/shard_map/ppermute | solution.py:26
  155.0 23.9 %collective-permute-start.27 = (bf16[16,8192]{1,0:T(8,128)(2,1)S(1)}, bf16[16,8192]{1,0:T(8,128)(2,1)S(1)}, u32[]{:S(2)}, u32[]{:S(2)}) collective-permute-start(bf16[16,8192]{1,0:T(8,128)(2,1)S(1)} %add_convert_fusion.9), channel_id=1, source_target_pairs={{0,17},{1,16},{2,19},{3,18},{4,21},{5,20},{6,23},{7,22},{8,25},{9,... | collective-permute-start | bytes 786440 | tf_op jit(solution)/shard_map/ppermute | solution.py:83
  162.3 16.6 %collective-permute-start.28 = (bf16[16,8192]{1,0:T(8,128)(2,1)S(1)}, bf16[16,8192]{1,0:T(8,128)(2,1)S(1)}, u32[]{:S(2)}, u32[]{:S(2)}) collective-permute-start(bf16[16,8192]{1,0:T(8,128)(2,1)S(1)} %fusion.3), channel_id=1, source_target_pairs={{0,16},{1,17},{2,18},{3,19},{4,20},{5,21},{6,22},{7,23},{8,24},{9,... | collective-permute-start | bytes 786440 | tf_op jit(solution)/shard_map/ppermute | solution.py:83
  164.2 14.7 %collective-permute-start.34 = (bf16[16,8192]{1,0:T(8,128)(2,1)S(1)}, bf16[16,8192]{1,0:T(8,128)(2,1)S(1)}, u32[]{:S(2)}, u32[]{:S(2)}) collective-permute-start(bf16[16,8192]{1,0:T(8,128)(2,1)S(1)} %add_convert_fusion.3), channel_id=1, source_target_pairs={{0,30},{1,31},{2,16},{3,17},{4,18},{5,19},{6,20},{7,21},{8,22},{9,... | collective-permute-start | bytes 786440 | tf_op jit(solution)/shard_map/ppermute | solution.py:83
  170.0 11.0 %collective-permute-start.35 = (bf16[16,8192]{1,0:T(8,128)(2,1)S(1)}, bf16[16,8192]{1,0:T(8,128)(2,1)S(1)}, u32[]{:S(2)}, u32[]{:S(2)}) collective-permute-start(bf16[16,8192]{1,0:T(8,128)(2,1)S(1)} %add_convert_fusion.1), channel_id=1, source_target_pairs={{0,18},{1,19},{2,20},{3,21},{4,22},{5,23},{6,24},{7,25},{8,26},{9,... | collective-permute-start | bytes 786440 | tf_op jit(solution)/shard_map/ppermute | solution.py:83
  (19 other events, 275.3 us)
Sparse Core Ops, SparseCore 0:
  15.4 53.0 all-gather.1
  100.6 51.8 reduce-scatter.1
